TPU v7x, 512 devices: a whole 4x8x8 slice. The times are simulated.
512 devices in a mesh: ctx: 64 (over z_hi, y, core), exp: 8 (over x, z_lo).
Axes of the slice: x: 4, y: 8, z: 8 (z_hi: 4, z_lo: 2; z = z_hi * 2 + z_lo), core: 2. Of those that a mesh axis runs over, the one named last changes fastest.
Arguments:
- residual: bfloat16 [65536, 2048], P(('ctx', 'exp')), may hold values from -6 to 6
- out_grad: bfloat16 [65536, 2048], P(('ctx', 'exp')), may hold values from -6 to 6
- norm_gain: bfloat16 [2048], replicated, may hold values from 0.25 to 1.75
- expert_ids: int32 [65536, 6], P(('ctx', 'exp')), may hold values from 0 to 63, as said below
- route_weights: bfloat16 [65536, 6], P(('ctx', 'exp')), may hold values from 0.19921875 to 1
- gate_up: bfloat16 [8, 2, 2048, 768], P('exp', None, 'ctx'), may hold values from -0.125 to 0.125
- down_proj: bfloat16 [8, 768, 2048], P('exp', 'ctx'), may hold values from -0.21875 to 0.21875
- out_proj: bfloat16 [1024, 2048], P('exp'), may hold values from -0.1875 to 0.1875
- queries: bfloat16 [65536, 1536], P('ctx', 'exp'), may hold values from -14 to 14
- keys_in: bfloat16 [65536, 1536], P('ctx', 'exp'), may hold values from -6 to 6
- values_in: bfloat16 [65536, 1024], P('ctx', 'exp'), may hold values from -6 to 6
- segments: int32 [65536], P('ctx'), may hold values from 0 to 255, never falling along the last dimension, each value on 1 to 512 neighbouring positions
Outputs:
- residual_grad: bfloat16 [65536, 2048], P(('ctx', 'exp'))
- query_grad: bfloat16 [65536, 1536], P('ctx', 'exp')
- key_grad: bfloat16 [65536, 1536], P('ctx', 'exp')
- value_grad: bfloat16 [65536, 1024], P('ctx', 'exp')
Inputs may be any that keep to these rules, and one draw needn't show every extreme that they name: `expert_ids`: each token names 6 different experts, exactly one of them below 8. Among the 128 tokens of one device at most 24 name any one expert below 8. `segments`: tokens of one document are consecutive; a document has at most 512 tokens.
All inputs are finite; a program needn't handle non-finite values.
Results may differ from a plain program's by a relative error of at most 0.029.
Values may be sent and summed in bfloat16 or wider, within the bound.
A program may use at most 128 MiB of HBM per device.

v0:
```python
import jax
import jax.numpy as jnp
from jax import lax
from jax.sharding import PartitionSpec as P

D = 2048
QK = 192
VD = 128
TOPK = 6


EPSILON = 1e-06
MASKED = -1e30


def shifted(value, axis, by):
    count = lax.axis_size(axis)
    pairs = [(i, i + by) for i in range(count) if 0 <= i + by < count]
    return lax.ppermute(value, axis, pairs)


def contract_last(left, right):
    return lax.dot_general(
        left, right, (((1,), (1,)), ((), ())), preferred_element_type=jnp.float32
    )


def route_table(expert_ids, route_weights, count, capacity):
    tokens = expert_ids.shape[0]
    wanted = jnp.arange(count, dtype=jnp.int32)
    onehot = (expert_ids[:, :, None] == wanted[None, None, :]).astype(jnp.int32)
    onehot = onehot.reshape(tokens * TOPK, count)
    before = jnp.cumsum(onehot, axis=0) - onehot
    target = jnp.sum(
        onehot * (jnp.arange(count, dtype=jnp.int32)[None, :] * capacity + before), axis=1
    )
    target = jnp.where(jnp.sum(onehot, axis=1) > 0, target, -1)
    slots = jnp.arange(count * capacity, dtype=jnp.int32)
    table = (target[None, :] == slots[:, None]).astype(jnp.float32)
    slot_gate = jnp.sum(table * route_weights.astype(jnp.float32).reshape(1, tokens * TOPK), axis=1)
    token_table = jnp.sum(table.reshape(count * capacity, tokens, TOPK), axis=2)
    return (token_table.astype(jnp.bfloat16), slot_gate.astype(jnp.bfloat16))


def swiglu_back(gate_pre, up_pre, hidden_grad):
    sigm = jax.nn.sigmoid(gate_pre)
    gate_grad = (hidden_grad * up_pre * sigm * (1.0 + gate_pre * (1.0 - sigm))).astype(jnp.bfloat16)
    up_grad = (hidden_grad * gate_pre * sigm).astype(jnp.bfloat16)
    return (gate_grad, up_grad)


def normalize(rows_in, gain_f):
    feats = rows_in.astype(jnp.float32)
    inverse = lax.rsqrt(jnp.mean(feats * feats, axis=1, keepdims=True) + EPSILON)
    return (feats, inverse, (feats * inverse * gain_f).astype(jnp.bfloat16))


def norm_back(feats, inverse, gain_f, normed_grad, grad_rows):
    scaled = normed_grad * gain_f
    cube = inverse * inverse * inverse
    total = (
        grad_rows.astype(jnp.float32)
        + inverse * scaled
        - feats * cube * jnp.mean(scaled * feats, axis=1, keepdims=True)
    )
    return total.astype(jnp.bfloat16)


def expert_rows(slot_in, slot_dy, slot_gate, gate_up, down_proj):
    gate_col = slot_gate.astype(jnp.float32)[:, None]
    full_gu, full_down = (
        lax.all_gather(gate_up, "ctx", axis=2, tiled=True),
        lax.all_gather(down_proj, "ctx", axis=1, tiled=True),
    )
    gate_pre = jnp.dot(slot_in, full_gu[0, 0], preferred_element_type=jnp.float32)
    up_pre = jnp.dot(slot_in, full_gu[0, 1], preferred_element_type=jnp.float32)
    hidden_grad = gate_col * contract_last(slot_dy, full_down[0])
    gate_grad, up_grad = swiglu_back(gate_pre, up_pre, hidden_grad)
    stash = full_gu[0]
    slot_out = contract_last(gate_grad, stash[0]) + contract_last(up_grad, stash[1])
    return slot_out.astype(jnp.bfloat16)


def score_block(query_heads, key_win, allowed):
    scores = jnp.einsum(
        "qhd,khd->hqk", query_heads, key_win, preferred_element_type=jnp.float32
    ) * QK ** (-0.5)
    return jnp.where(allowed[None], scores, MASKED)


def forward_stats(query_heads, key_win, value_win, allowed):
    scores = score_block(query_heads, key_win, allowed)
    top = jnp.max(scores, axis=2, keepdims=True)
    lse = top + jnp.log(jnp.sum(jnp.exp(scores - top), axis=2, keepdims=True))
    probs_low = jnp.exp(scores - lse).astype(jnp.bfloat16)
    attended = jnp.einsum(
        "hqk,khd->qhd", probs_low, value_win, preferred_element_type=jnp.float32
    ).astype(jnp.bfloat16)
    return (lse, attended)


def backward_grads(query_heads, key_win, value_win, allowed, lse, attended, grad_heads):
    probs = jnp.exp(score_block(query_heads, key_win, allowed) - lse)
    probs_low = probs.astype(jnp.bfloat16)
    delta = jnp.sum(grad_heads.astype(jnp.float32) * attended.astype(jnp.float32), axis=2)
    value_part = jnp.einsum(
        "hqk,qhd->khd", probs_low, grad_heads, preferred_element_type=jnp.float32
    )
    prob_grad = jnp.einsum(
        "qhd,khd->hqk", grad_heads, value_win, preferred_element_type=jnp.float32
    )
    score_grad = (probs * (prob_grad - jnp.transpose(delta)[:, :, None])).astype(jnp.bfloat16)
    query_part = jnp.einsum(
        "hqk,khd->qhd", score_grad, key_win, preferred_element_type=jnp.float32
    ) * QK ** (-0.5)
    key_part = jnp.einsum(
        "hqk,qhd->khd", score_grad, query_heads, preferred_element_type=jnp.float32
    ) * QK ** (-0.5)
    return (query_part, key_part, value_part)


def shards(
    residual,
    out_grad,
    norm_gain,
    expert_ids,
    route_weights,
    gate_up,
    down_proj,
    out_proj,
    queries,
    keys_in,
    values_in,
    segments,
):
    ctx_index = lax.axis_index("ctx")
    tokens = queries.shape[0]
    heads_here = queries.shape[1] // QK
    reach = tokens // 2
    width = reach + tokens
    query_heads = queries.reshape(tokens, heads_here, QK)
    far_keys, far_values, far_segs = shifted(
        (keys_in[tokens - reach :], values_in[tokens - reach :], segments[tokens - reach :]),
        "ctx",
        1,
    )
    key_win = jnp.concatenate([far_keys, keys_in], axis=0).reshape(width, heads_here, QK)
    value_win = jnp.concatenate([far_values, values_in], axis=0).reshape(width, heads_here, VD)
    seg_win = jnp.concatenate([far_segs, segments], axis=0)
    query_pos = ctx_index * tokens + jnp.arange(tokens, dtype=jnp.int32)
    key_pos = ctx_index * tokens - reach + jnp.arange(width, dtype=jnp.int32)
    allowed = (
        (segments[:, None] == seg_win[None, :])
        & (key_pos[None, :] <= query_pos[:, None])
        & (key_pos[None, :] >= 0)
    )
    lse, attended = forward_stats(query_heads, key_win, value_win, allowed)
    gain_f = norm_gain.astype(jnp.float32)
    n_exp = lax.axis_size("exp")
    tok_dev = residual.shape[0]
    capacity = 3 * tok_dev // (2 * n_exp)
    feats, inverse, normed = normalize(residual, gain_f)
    table, slot_gate = route_table(expert_ids, route_weights, n_exp, capacity)
    slot_in = jnp.dot(table, normed, preferred_element_type=jnp.float32).astype(jnp.bfloat16)
    slot_dy = jnp.dot(table, out_grad, preferred_element_type=jnp.float32).astype(jnp.bfloat16)
    recv_in, recv_dy, recv_gate = (
        lax.all_to_all(
            slot_in.reshape(n_exp, capacity, D), "exp", split_axis=0, concat_axis=0, tiled=True
        ),
        lax.all_to_all(
            slot_dy.reshape(n_exp, capacity, D), "exp", split_axis=0, concat_axis=0, tiled=True
        ),
        lax.all_to_all(
            slot_gate.reshape(n_exp, capacity), "exp", split_axis=0, concat_axis=0, tiled=True
        ),
    )
    slot_out = expert_rows(
        recv_in.reshape(n_exp * capacity, D),
        recv_dy.reshape(n_exp * capacity, D),
        recv_gate.reshape(n_exp * capacity),
        gate_up,
        down_proj,
    )
    returned = lax.all_to_all(
        slot_out.reshape(n_exp, capacity, D), "exp", split_axis=0, concat_axis=0, tiled=True
    )
    normed_grad = lax.dot_general(
        table,
        returned.reshape(n_exp * capacity, D),
        (((0,), (0,)), ((), ())),
        preferred_element_type=jnp.float32,
    )
    residual_grad = norm_back(feats, inverse, gain_f, normed_grad, out_grad)
    head_grad = contract_last(
        lax.all_gather(residual_grad, "exp", axis=0, tiled=True), out_proj
    ).astype(jnp.bfloat16)
    again_keys, again_values = shifted(
        (keys_in[tokens - reach :], values_in[tokens - reach :]), "ctx", 1
    )
    key_back = jnp.concatenate([again_keys, keys_in], axis=0).reshape(width, heads_here, QK)
    value_back = jnp.concatenate([again_values, values_in], axis=0).reshape(width, heads_here, VD)
    grad_heads = head_grad.reshape(tokens, heads_here, VD)
    query_part, key_part, value_part = backward_grads(
        query_heads, key_back, value_back, allowed, lse, attended, grad_heads
    )
    key_flat = key_part.reshape(width, heads_here * QK)
    value_flat = value_part.reshape(width, heads_here * VD)
    home_keys, home_values = shifted(
        (key_flat[:reach].astype(jnp.bfloat16), value_flat[:reach].astype(jnp.bfloat16)), "ctx", -1
    )
    key_lead = jnp.zeros((tokens - reach, heads_here * QK), jnp.float32)
    value_lead = jnp.zeros((tokens - reach, heads_here * VD), jnp.float32)
    key_total = key_flat[reach:] + jnp.concatenate(
        [key_lead, home_keys.astype(jnp.float32)], axis=0
    )
    value_total = value_flat[reach:] + jnp.concatenate(
        [value_lead, home_values.astype(jnp.float32)], axis=0
    )
    query_grad = query_part.reshape(tokens, heads_here * QK).astype(jnp.bfloat16)
    return (
        residual_grad,
        query_grad,
        key_total.astype(jnp.bfloat16),
        value_total.astype(jnp.bfloat16),
    )


def solution(mesh):
    return jax.shard_map(
        shards,
        mesh=mesh,
        in_specs=(
            P(("ctx", "exp"), None),
            P(("ctx", "exp"), None),
            P(),
            P(("ctx", "exp"), None),
            P(("ctx", "exp"), None),
            P("exp", None, "ctx", None),
            P("exp", "ctx", None),
            P("exp", None),
            P("ctx", "exp"),
            P("ctx", "exp"),
            P("ctx", "exp"),
            P("ctx"),
        ),
        out_specs=(P(("ctx", "exp"), None), P("ctx", "exp"), P("ctx", "exp"), P("ctx", "exp")),
        check_vma=False,
    )
```

profile of v0, /device:TPU:57, one launch (start us, length us, event | category | flops | bytes accessed | tf_op | source)
XLA Modules:
  0.0 359.6 jit_solution(14266020847080110006)
XLA Ops:
  14.7 5.8 %all-to-all-start = ((bf16[8,1,24]{2,1,0:T(2,128)(2,1)}), bf16[8,1,24]{2,1,0:T(2,128)(2,1)S(1)}, u32[]{:S(2)}, u32[]{:S(2)}) async-start(bf16[8,1,24]{2,1,0:T(2,128)(2,1)} %convert_element_type.169), calls=%async_computation | async-start | bytes 8192 | tf_op jit(solution)/shard_map/all_to_all | solution.py:173
  20.9 2.3 convolution_convert_fusion.1
  23.1 2.4 all-to-all-done
  25.5 3.5 all-to-all-start.1
  31.0 2.4 convolution_convert_fusion
  33.4 7.6 %all-to-all-done.1 = bf16[8,24,2048]{2,1,0:T(8,128)(2,1)S(1)} async-done(((bf16[8,24,2048]{2,1,0:T(8,128)(2,1)}), bf16[8,24,2048]{2,1,0:T(8,128)(2,1)S(1)}, u32[]{:S(2)}, u32[]{:S(2)}) %all-to-all-start.1) | async-done | bytes 786464 | tf_op jit(solution)/shard_map/all_to_all | solution.py:170
  41.0 3.5 all-to-all-start.2
  44.7 65.5 %all-gather.4.cloned.1.call-done = bf16[1,768,2048]{2,0,1:T(2,128)(2,1)} async-done(((bf16[1,12,2048]{2,0,1:T(2,128)(2,1)}), bf16[1,768,2048]{2,0,1:T(2,128)(2,1)}) %all-gather.4.cloned.1.call-update) | async-done | bytes 3145744 | tf_op jit(solution)/shard_map/all_gather | solution.py:73
  110.3 5.7 %fusion.13 = f32[192,768]{1,0:T(8,128)} fusion(bf16[192,2048]{1,0:T(8,128)(2,1)S(1)} %bitcast.114, bf16[1,768,2048]{2,0,1:T(2,128)(2,1)} %all-gather.4.cloned.1.call-done, f32[192]{0:T(256)S(1)} %reshape.232), kind=kOutput, calls=%fused_computation.29 | convolution fusion | flops 604127232 | bytes 4522752 | tf_op jit(solution)/shard_map/dot_general | solution.py:23
  116.0 88.3 %all-gather.6.cloned.1.call-done = bf16[1,2,2048,768]{3,2,1,0:T(8,128)(2,1)} async-done(((bf16[1,2,32,768]{3,2,1,0:T(8,128)(2,1)}), bf16[1,2,2048,768]{3,2,1,0:T(8,128)(2,1)}) %all-gather.6.cloned.1.call-update) | async-done | bytes 6291472 | tf_op jit(solution)/shard_map/all_gather | solution.py:72
  204.3 2.7 fusion.7
  207.9 4.4 %fusion.4 = f32[192,2048]{1,0:T(8,128)} fusion(bf16[1,2,2048,768]{3,2,1,0:T(8,128)(2,1)} %all-gather.6.cloned.1.call-done, f32[192,768]{1,0:T(8,128)} %fusion.13, f32[192,768]{1,0:T(8,128)S(1)} %fusion.7), kind=kOutput, calls=%fused_computation.10 | convolution fusion | flops 604864512 | bytes 5898240 | tf_op jit(solution)/shard_map/dot_general | solution.py:23
  212.3 5.7 %fusion.10 = bf16[192,2048]{1,0:T(8,128)(2,1)S(1)} fusion(f32[192,2048]{1,0:T(8,128)} %fusion.4, bf16[1,2,2048,768]{3,2,1,0:T(8,128)(2,1)} %all-gather.6.cloned.1.call-done, f32[192,768]{1,0:T(8,128)} %fusion.13, bf16[192,2048]{1,0:T(8,128)(2,1)S(1)} %bitcast.116, f32[192,768]{1,0:T(8,128)} %copy-done.9), kind=kOutput, calls=%fused_computation.17 | convolution fusion | flops 1210220544 | bytes 10616832 | tf_op jit(solution)/shard_map/dot_general | solution.py:23
  218.0 16.0 %all_to_all.21 = bf16[8,24,2048]{2,1,0:T(8,128)(2,1)S(1)} all-to-all(bf16[8,24,2048]{2,1,0:T(8,128)(2,1)S(1)} %bitcast.117), channel_id=1, replica_groups=mesh['ctx'=64,'exp'=8] {'exp'}, dimensions={0} | all-to-all | bytes 1572864 | tf_op jit(solution)/shard_map/all_to_all | solution.py:184
  235.7 7.1 %collective-permute-start = (bf16[512,192]{0,1:T(8,128)(2,1)S(1)}, bf16[512,192]{0,1:T(8,128)(2,1)S(1)}, u32[]{:S(2)}, u32[]{:S(2)}) collective-permute-start(bf16[512,192]{0,1:T(8,128)(2,1)S(1)} %slice.53), channel_id=1, source_target_pairs={{0,8},{8,16},{16,24},{24,32},{32,40},{40,48},{48,56},{56,64},{64,7... | collective-permute-start | bytes 589832 | tf_op jit(solution)/shard_map/ppermute | solution.py:19
  244.8 3.1 collective-permute-start.2
  249.8 2.3 fusion.57
  252.1 2.7 copy-done.1
  255.6 72.1 %all-gather.8.cloned.1.call-done = bf16[1024,2048]{1,0:T(8,128)(2,1)} async-done(((bf16[128,2048]{1,0:T(8,128)(2,1)}), bf16[1024,2048]{1,0:T(8,128)(2,1)}) %all-gather.8.cloned.1.call-update) | async-done | bytes 4194320 | tf_op jit(solution)/shard_map/all_gather | solution.py:195
  327.7 3.8 %convolution_convert_fusion.3 = bf16[1024,128]{0,1:T(8,128)(2,1)S(1)} fusion(bf16[1024,2048]{1,0:T(8,128)(2,1)} %all-gather.8.cloned.1.call-done, bf16[128,2048]{1,0:T(8,128)(2,1)S(1)} %copy-done), kind=kOutput, calls=%fused_computation.35 | convolution fusion | flops 537001984 | bytes 4980736 | tf_op jit(solution)/shard_map/dot_general | solution.py:23
  338.2 2.8 collective-permute-start.4
  341.0 2.6 collective-permute-start.3
  343.6 3.9 %collective-permute-done.4 = bf16[512,128]{0,1:T(8,128)(2,1)S(1)} collective-permute-done((bf16[512,128]{0,1:T(8,128)(2,1)S(1)}, bf16[512,128]{0,1:T(8,128)(2,1)S(1)}, u32[]{:S(2)}, u32[]{:S(2)}) %collective-permute-start.4) | collective-permute-done | bytes 131104 | tf_op jit(solution)/shard_map/ppermute | solution.py:19
  348.4 3.9 %collective-permute-done.3 = bf16[512,192]{0,1:T(8,128)(2,1)S(1)} collective-permute-done((bf16[512,192]{0,1:T(8,128)(2,1)S(1)}, bf16[512,192]{0,1:T(8,128)(2,1)S(1)}, u32[]{:S(2)}, u32[]{:S(2)}) %collective-permute-start.3) | collective-permute-done | bytes 196640 | tf_op jit(solution)/shard_map/ppermute | solution.py:19
  (81 shorter events, 25.3 us)
Async XLA Ops:
  7.2 320.6 %copy-start = (bf16[128,2048]{1,0:T(8,128)(2,1)S(1)}, bf16[128,2048]{1,0:T(8,128)(2,1)}, u32[]{:S(2)}) copy-start(bf16[128,2048]{1,0:T(8,128)(2,1)} %param.19) | copy-start | bytes 1572868
  7.2 103.1 %all-gather.4.cloned.1.call-start = ((), (), s32[]{:S(2)}) async-start(), calls=%async_computation.4 | async-start | bytes 6389760 | tf_op jit(solution)/shard_map/all_gather | solution.py:73
  8.9 195.5 %all-gather.6.cloned.1.call-start = ((), (), s32[]{:S(2)}) async-start(), calls=%async_computation.5 | async-start | bytes 6389760 | tf_op jit(solution)/shard_map/all_gather | solution.py:72
  14.7 10.8 %all-to-all-start = ((bf16[8,1,24]{2,1,0:T(2,128)(2,1)}), bf16[8,1,24]{2,1,0:T(2,128)(2,1)S(1)}, u32[]{:S(2)}, u32[]{:S(2)}) async-start(bf16[8,1,24]{2,1,0:T(2,128)(2,1)} %convert_element_type.169), calls=%async_computation | async-start | bytes 8192 | tf_op jit(solution)/shard_map/all_to_all | solution.py:173
  25.5 15.5 %all-to-all-start.1 = ((bf16[8,24,2048]{2,1,0:T(8,128)(2,1)}), bf16[8,24,2048]{2,1,0:T(8,128)(2,1)S(1)}, u32[]{:S(2)}, u32[]{:S(2)}) async-start(bf16[8,24,2048]{2,1,0:T(8,128)(2,1)} %bitcast.3), calls=%async_computation.1 | async-start | bytes 1572864 | tf_op jit(solution)/shard_map/all_to_all | solution.py:170
  41.0 75.0 %all-to-all-start.2 = ((bf16[8,24,2048]{2,1,0:T(8,128)(2,1)}), bf16[8,24,2048]{2,1,0:T(8,128)(2,1)S(1)}, u32[]{:S(2)}, u32[]{:S(2)}) async-start(bf16[8,24,2048]{2,1,0:T(8,128)(2,1)} %bitcast.5), calls=%async_computation.2 | async-start | bytes 1572864 | tf_op jit(solution)/shard_map/all_to_all | solution.py:167
  44.6 283.2 %all-gather.8.cloned.1.call-start = ((), (), s32[]{:S(2)}) async-start(), calls=%async_computation.6 | async-start | bytes 4718592 | tf_op jit(solution)/shard_map/all_gather | solution.py:195
  207.0 0.9 copy-start.9
  212.3 21.7 %copy-start.3 = (bf16[128,2048]{1,0:T(8,128)(2,1)S(1)}, bf16[128,2048]{1,0:T(8,128)(2,1)}, u32[]{:S(2)}) copy-start(bf16[128,2048]{1,0:T(8,128)(2,1)} %param.12) | copy-start | bytes 1572868
  212.3 22.2 %copy-start.4 = (bf16[128,2048]{1,0:T(8,128)(2,1)S(1)}, bf16[128,2048]{1,0:T(8,128)(2,1)}, u32[]{:S(2)}) copy-start(bf16[128,2048]{1,0:T(8,128)(2,1)} %param.13) | copy-start | bytes 1572868
  217.9 17.7 %copy-start.5 = (bf16[1024,192]{0,1:T(8,128)(2,1)S(1)}, bf16[1024,192]{0,1:T(8,128)(2,1)}, u32[]{:S(2)}) copy-start(bf16[1024,192]{0,1:T(8,128)(2,1)} %param.21) | copy-start | bytes 1179652
  217.9 24.9 %copy-start.7 = (s32[1024]{0:T(1024)S(1)}, s32[1024]{0:T(1024)}, u32[]{:S(2)}) copy-start(s32[1024]{0:T(1024)} %param.23) | copy-start | bytes 12292
  218.0 26.8 %copy-start.6 = (bf16[1024,128]{1,0:T(8,128)(2,1)S(1)}, bf16[1024,128]{1,0:T(8,128)(2,1)}, u32[]{:S(2)}) copy-start(bf16[1024,128]{1,0:T(8,128)(2,1)} %param.22) | copy-start | bytes 786436
  234.0 15.7 %copy-start.8 = (bf16[1024,192]{0,1:T(8,128)(2,1)S(1)}, bf16[1024,192]{0,1:T(8,128)(2,1)}, u32[]{:S(2)}) copy-start(bf16[1024,192]{0,1:T(8,128)(2,1)} %param.20) | copy-start | bytes 1179652
  235.7 14.0 %collective-permute-start = (bf16[512,192]{0,1:T(8,128)(2,1)S(1)}, bf16[512,192]{0,1:T(8,128)(2,1)S(1)}, u32[]{:S(2)}, u32[]{:S(2)}) collective-permute-start(bf16[512,192]{0,1:T(8,128)(2,1)S(1)} %slice.53), channel_id=1, source_target_pairs={{0,8},{8,16},{16,24},{24,32},{32,40},{40,48},{48,56},{56,64},{64,7... | collective-permute-start | bytes 589832 | tf_op jit(solution)/shard_map/ppermute | solution.py:19
  242.8 5.1 %collective-permute-start.1 = (s32[512]{0:T(512)S(1)}, s32[512]{0:T(512)S(1)}, u32[]{:S(2)}, u32[]{:S(2)}) collective-permute-start(s32[512]{0:T(512)S(1)} %slice.54), channel_id=1, source_target_pairs={{0,8},{8,16},{16,24},{24,32},{32,40},{40,48},{48,56},{56,64},{64,7... | collective-permute-start | bytes 6152 | tf_op jit(solution)/shard_map/ppermute | solution.py:19
  244.8 4.8 %collective-permute-start.2 = (bf16[512,128]{1,0:T(8,128)(2,1)S(1)}, bf16[512,128]{1,0:T(8,128)(2,1)S(1)}, u32[]{:S(2)}, u32[]{:S(2)}) collective-permute-start(bf16[512,128]{1,0:T(8,128)(2,1)S(1)} %slice.55), channel_id=1, source_target_pairs={{0,8},{8,16},{16,24},{24,32},{32,40},{40,48},{48,56},{56,64},{64,7... | collective-permute-start | bytes 393224 | tf_op jit(solution)/shard_map/ppermute | solution.py:19
  252.1 2.7 copy-start.1
  327.7 4.0 %copy-start.2 = (f32[1024,1536]{0,1:T(8,128)S(1)}, f32[1024,1536]{0,1:T(8,128)}, u32[]{:S(2)}) copy-start(f32[1024,1536]{0,1:T(8,128)} %copy-done.1) | copy-start | bytes 18874372
  338.2 9.3 %collective-permute-start.4 = (bf16[512,128]{0,1:T(8,128)(2,1)S(1)}, bf16[512,128]{0,1:T(8,128)(2,1)S(1)}, u32[]{:S(2)}, u32[]{:S(2)}) collective-permute-start(bf16[512,128]{0,1:T(8,128)(2,1)S(1)} %fusion.47), channel_id=1, source_target_pairs={{8,0},{16,8},{24,16},{32,24},{40,32},{48,40},{56,48},{64,56},{72,6... | collective-permute-start | bytes 393224 | tf_op jit(solution)/shard_map/ppermute | solution.py:19
  341.0 11.2 %collective-permute-start.3 = (bf16[512,192]{0,1:T(8,128)(2,1)S(1)}, bf16[512,192]{0,1:T(8,128)(2,1)S(1)}, u32[]{:S(2)}, u32[]{:S(2)}) collective-permute-start(bf16[512,192]{0,1:T(8,128)(2,1)S(1)} %fusion.46), channel_id=1, source_target_pairs={{8,0},{16,8},{24,16},{32,24},{40,32},{48,40},{56,48},{64,56},{72,6... | collective-permute-start | bytes 589832 | tf_op jit(solution)/shard_map/ppermute | solution.py:19
Sparse Core Ops, SparseCore 0:
  11.9 98.3 all-gather.3
  113.7 90.6 all-gather.5
  235.8 91.9 all-gather.7
where the time goes:
time: 361 us; the launch traced here: 360 us
  waiting for transfers between devices  246 us (68%)
  matrix products  36.1 us (10%)
  starting transfers between devices  30.6 us (8%)
  blocking collectives  16 us (4%)
  between operations  14.1 us (4%)
  local copies, waits for them, and re-layouts  9.58 us (3%)
  other arithmetic  7.12 us (2%)
    all_gather x1, waiting for transfers between devices, expert_rows(): lax.all_gather(gate_up, 'ctx', axis=2, tiled=True)  88.3 us
    all_gather x1, waiting for transfers between devices, shards(): lax.all_gather(residual_grad, 'exp', axis=0, tiled=True)  72.1 us
    all_gather x1, waiting for transfers between devices, expert_rows(): lax.all_gather(down_proj, 'ctx', axis=1, tiled=True)  65.5 us
    dot_general x4, matrix products, contract_last(): lax.dot_general(left, right, (((1,), (1,)), ((), ())), preferred_element_...  19.6 us
    ppermute x5, starting transfers between devices, shifted(): return lax.ppermute(value, axis, pairs)  17.5 us
    all_to_all x1, blocking collectives, shards(): lax.all_to_all(slot_out.reshape(n_exp, capacity, D), 'exp', split_axis=0,...  16 us
    ppermute x5, waiting for transfers between devices, shifted(): return lax.ppermute(value, axis, pairs)  9.43 us
    all_to_all x1, waiting for transfers between devices, shards(): lax.all_to_all(slot_dy.reshape(n_exp, capacity, D), 'exp', split_axis=0,...  7.6 us
  transfers between devices with their start and end apart: 11, of which 8 were waited for; matrix products, arithmetic and copies ran while one was open for 6% of the time, Pallas kernels for 0%

commit v1 on v0

v1 whole, which is shorter than its diff:
```python
import functools

import jax
import jax.numpy as jnp
from jax import lax
from jax.experimental import pallas as pl
from jax.experimental.pallas import tpu as pltpu
from jax.sharding import PartitionSpec as P

D = 2048
QK = 192
VD = 128
FF = 768
TOPK = 6
N_EXP = 8
N_CTX = 64
NH = 4
NY = 8
TOK = 1024
REACH = 512
TOK_DEV = 128
CAP = 24
SLOTS = 48
SHARD = 96
QB = 256
WIN = QB + REACH
N_QB = TOK // QB
EPSILON = 1e-06
MASKED = -1e30
SCALE = QK ** (-0.5)
BF = jnp.bfloat16
F32 = jnp.float32
MESH = pl.DeviceIdType.MESH


def dot_nn(a, b):
    return lax.dot_general(a, b, (((1,), (0,)), ((), ())), preferred_element_type=F32)


def dot_nt(a, b):
    return lax.dot_general(a, b, (((1,), (1,)), ((), ())), preferred_element_type=F32)


def dot_tn(a, b):
    return lax.dot_general(a, b, (((0,), (0,)), ((), ())), preferred_element_type=F32)


def scratch():
    vm, dma = pltpu.VMEM, pltpu.SemaphoreType.DMA
    return dict(
        w=vm((N_CTX, SHARD, FF), BF),
        opf=vm((N_EXP, VD, D), BF),
        lhs=vm((2 * TOK_DEV, D), BF),
        xs=vm((N_EXP, SLOTS, D), BF),
        xr=vm((N_EXP, SLOTS, D), BF),
        sel=vm((NH, 2, 256, FF), BF),
        pre=vm((256, 2 * FF), F32),
        hid=vm((256, FF), F32),
        gg=vm((192, 2 * FF), BF),
        os=vm((2, N_EXP, SLOTS, 512), BF),
        orr=vm((2, N_EXP, SLOTS, 512), BF),
        tin=vm((TOK_DEV, N_EXP * SLOTS), BF),
        tdy=vm((TOK_DEV, N_EXP * SLOTS), BF),
        inv=vm((TOK_DEV, 1), F32),
        ng=vm((TOK_DEV, D), F32),
        hs=vm((N_EXP, TOK_DEV, VD), BF),
        hr=vm((N_EXP, TOK_DEV, VD), BF),
        kw=vm((REACH + TOK, QK), BF),
        vw=vm((REACH + TOK, VD), BF),
        segh=vm((8, 128), jnp.int32),
        probs=vm((N_QB, QB, WIN), F32),
        plt=vm((N_QB, WIN, QB), BF),
        att=vm((TOK, VD), F32),
        dk=vm((REACH + TOK, QK), F32),
        dv=vm((REACH + TOK, VD), F32),
        ks=vm((REACH, QK), BF),
        vs=vm((REACH, VD), BF),
        kr=vm((REACH, QK), BF),
        vr=vm((REACH, VD), BF),
        s_local=dma((8,)),
        s_wsend=dma,
        s_w=dma((NH * NY,)),
        s_cross=dma((NH,)),
        s_halo_s=dma((3,)),
        s_halo_r=dma((3,)),
        s_op_s=dma,
        s_op_r=dma((4,)),
        s_x=dma((2,)),
        s_o=dma((4,)),
        s_h=dma((2,)),
        s_k=dma((4,)),
    )


NAMES = tuple(scratch())


def body(
    w_in, op_in, keys_in, values_in, res, dy, gain, ids, rw, seg, q,
    out_res, out_q, out_k, out_v, *rest,
):
    s = dict(zip(NAMES, rest))
    ctx, me = lax.axis_index("ctx"), lax.axis_index("exp")
    h, y, c = ctx // 16, (ctx // 2) % NY, ctx % 2
    x, l = me // 2, me % 2

    def at(hh, yy):
        return (hh * NY + yy) * 2 + c

    sibling = (ctx + 1 - 2 * c, me)
    up = (at(h, (y + 1) % NY), me)
    down = (at(h, (y + NY - 1) % NY), me)
    zs = [(at((h + k) % NH, y), me) for k in range(1, NH)]
    after = ((ctx + 1) % N_CTX, me)
    before = ((ctx + N_CTX - 1) % N_CTX, me)
    exps = [(ctx, (me + k) % N_EXP) for k in range(1, N_EXP)]
    lmate = (ctx, 2 * x + 1 - l)
    xmates = [(ctx, 2 * ((x + k) % 4) + l) for k in (2, 1, 3)]

    def send(src, dst, ssem, rsem, dev):
        pltpu.make_async_remote_copy(
            src_ref=src, dst_ref=dst, send_sem=ssem, recv_sem=rsem,
            device_id=dev, device_id_type=MESH,
        ).start()

    def wait(ref, sem):
        pltpu.make_async_copy(ref, ref, sem).wait()

    partners = [sibling, up, down, after, before] + zs + exps
    barrier = pltpu.get_barrier_semaphore()
    for dev in partners:
        pl.semaphore_signal(barrier, inc=1, device_id=dev, device_id_type=MESH)
    local = [
        pltpu.make_async_copy(w_in, s["w"].at[ctx], s["s_local"].at[0]),
        pltpu.make_async_copy(op_in, s["opf"].at[me], s["s_local"].at[1]),
        pltpu.make_async_copy(keys_in, s["kw"].at[pl.ds(REACH, TOK)], s["s_local"].at[2]),
        pltpu.make_async_copy(values_in, s["vw"].at[pl.ds(REACH, TOK)], s["s_local"].at[3]),
    ]
    for copy in local:
        copy.start()
    pl.semaphore_wait(barrier, len(partners))

    def wsend(src, hh, yy, dev):
        j = at(hh, yy)
        send(src, s["w"].at[j], s["s_wsend"], s["s_w"].at[hh * NY + yy], dev)

    def cross(src, hh, yy):
        send(src, s["w"].at[at(hh, yy)], s["s_wsend"], s["s_cross"].at[hh], sibling)

    wsend(w_in, h, y, up)
    wsend(w_in, h, y, down)
    for dev in zs:
        wsend(w_in, h, y, dev)
    cross(w_in, h, y)
    half = pl.ds(64 * c, 64)
    send(op_in.at[half], s["opf"].at[me, half], s["s_op_s"], s["s_op_r"].at[0], lmate)
    send(keys_in.at[pl.ds(REACH, REACH)], s["kw"].at[pl.ds(0, REACH)],
         s["s_halo_s"].at[0], s["s_halo_r"].at[0], after)
    send(values_in.at[pl.ds(REACH, REACH)], s["vw"].at[pl.ds(0, REACH)],
         s["s_halo_s"].at[1], s["s_halo_r"].at[1], after)
    send(seg, s["segh"], s["s_halo_s"].at[2], s["s_halo_r"].at[2], after)

    gain_f = gain[...].astype(F32)
    for r in range(0, TOK_DEV, 16):
        rows = pl.ds(r, 16)
        feats = res[rows, :].astype(F32)
        inverse = lax.rsqrt(jnp.mean(feats * feats, axis=1, keepdims=True) + EPSILON)
        s["inv"][rows, :] = inverse
        s["lhs"][rows, :] = (feats * inverse * gain_f).astype(BF)
    s["lhs"][pl.ds(TOK_DEV, TOK_DEV), :] = dy[...]

    ids_v = ids[...]
    live = ids_v < N_EXP
    expert = jnp.sum(jnp.where(live, ids_v, 0), axis=1, keepdims=True)
    weight = jnp.sum(jnp.where(live, rw[...].astype(F32), 0.0), axis=1, keepdims=True)
    lane = lax.broadcasted_iota(jnp.int32, (TOK_DEV, 128), 1)
    row = lax.broadcasted_iota(jnp.int32, (TOK_DEV, 128), 0)
    onehot = jnp.where(lane == expert, 1.0, 0.0)
    earlier = jnp.where(lane < row, 1.0, 0.0).astype(BF)
    counts = dot_nn(earlier, onehot.astype(BF))
    rank = jnp.sum(onehot * counts, axis=1, keepdims=True).astype(jnp.int32)
    place_in = expert * SLOTS + jnp.where(rank < 16, rank, rank + 16)
    place_dy = expert * SLOTS + jnp.where(rank < 16, rank + 16, rank + 24)
    slot = lax.broadcasted_iota(jnp.int32, (TOK_DEV, N_EXP * SLOTS), 1)
    hit_in = slot == place_in
    hit_dy = slot == place_dy
    s["tin"][...] = jnp.where(hit_in, weight, 0.0).astype(BF)
    s["tdy"][...] = jnp.where(hit_dy, weight, 0.0).astype(BF)
    table = jnp.concatenate(
        [jnp.where(hit_in, 1.0, 0.0).astype(BF), jnp.where(hit_dy, 1.0, 0.0).astype(BF)], axis=0
    )
    for col in range(0, D, 512):
        picked = dot_tn(table, s["lhs"][:, col : col + 512])
        s["xs"][:, :, col : col + 512] = picked.astype(BF).reshape(N_EXP, SLOTS, 512)
    for dev in exps:
        send(s["xs"].at[dev[1]], s["xr"].at[me], s["s_x"].at[0], s["s_x"].at[1], dev)
    own_x = pltpu.make_async_copy(s["xs"].at[me], s["xr"].at[me], s["s_local"].at[4])
    own_x.start()
    for dev in xmates:
        send(op_in.at[half], s["opf"].at[me, half], s["s_op_s"], s["s_op_r"].at[1], dev)

    def selection(k):
        hh = (h + k) % NH
        i = lax.broadcasted_iota(jnp.int32, (256, FF), 0)
        f = lax.broadcasted_iota(jnp.int32, (256, FF), 1)
        m = i % 16
        base = 192 * hh + 12 * (i // 16)
        first = base + jnp.where(m < 12, m, 3 * (m - 12))
        second = base + jnp.where(m >= 12, 3 * (m - 12) + 1, jnp.where(m >= 8, 3 * (m - 8) + 2, -9999))
        s["sel"][k, 0] = jnp.where(f == first, 1.0, 0.0).astype(BF)
        s["sel"][k, 1] = jnp.where(f == second, 1.0, 0.0).astype(BF)

    def halo_ready():
        wait(s["kw"].at[pl.ds(0, REACH)], s["s_halo_r"].at[0])
        wait(s["vw"].at[pl.ds(0, REACH)], s["s_halo_r"].at[1])
        wait(s["segh"], s["s_halo_r"].at[2])
        local[2].wait()
        local[3].wait()

    def seg_row(r):
        return s["segh"][4 + r : 5 + r, :] if r < 4 else seg[r - 4 : r - 3, :]

    def forward(b):
        seg_cols = jnp.transpose(seg[...].astype(F32)).astype(jnp.int32)
        seg_q = jnp.concatenate([seg_cols[:, 2 * b : 2 * b + 1], seg_cols[:, 2 * b + 1 : 2 * b + 2]], axis=0)
        pos_q = lax.broadcasted_iota(jnp.int32, (QB, 128), 0) + REACH
        pos_k = lax.broadcasted_iota(jnp.int32, (QB, 128), 1)
        scores = dot_nt(q[pl.ds(QB * b, QB), :], s["kw"][pl.ds(QB * b, WIN), :]) * SCALE
        pieces = []
        for t in range(WIN // 128):
            allowed = (seg_q == seg_row(2 * b + t)) & (pos_k + 128 * t <= pos_q)
            if 2 * b + t < 4:
                allowed = allowed & (ctx > 0)
            pieces.append(jnp.where(allowed, scores[:, 128 * t : 128 * t + 128], MASKED))
        scores = jnp.concatenate(pieces, axis=1)
        top = jnp.max(scores, axis=1, keepdims=True)
        raw = jnp.exp(scores - top)
        probs = raw / jnp.sum(raw, axis=1, keepdims=True)
        low = probs.astype(BF)
        s["probs"][b] = probs
        s["plt"][b] = jnp.transpose(low)
        s["att"][pl.ds(QB * b, QB), :] = (
            dot_nn(low, s["vw"][pl.ds(QB * b, WIN), :]).astype(BF).astype(F32)
        )

    def op_pass():
        wait(s["opf"].at[0, pl.ds(0, 64)], s["s_op_r"].at[0])
        other = lmate[1]
        for dev in xmates:
            send(s["opf"].at[other, half], s["opf"].at[other, half], s["s_op_s"], s["s_op_r"].at[2], dev)
        send(s["opf"].at[other, half], s["opf"].at[other, half], s["s_op_s"], s["s_op_r"].at[3], sibling)

    def op_cross(k, parity):
        wait(s["opf"].at[pl.ds(0, 3), pl.ds(0, 64)], s["s_op_r"].at[k])
        for step in (1, 2, 3):
            e = 2 * ((x + step) % 4) + parity
            send(s["opf"].at[e, half], s["opf"].at[e, half], s["s_op_s"], s["s_op_r"].at[3], sibling)

    def arrive(d, k):
        hh = (h + k) % NH
        if d == 0:
            if k > 0:
                wait(s["w"].at[0], s["s_w"].at[hh * NY + y])
                src = s["w"].at[at(hh, y)]
                wsend(src, hh, y, up)
                wsend(src, hh, y, down)
                cross(src, hh, y)
            return
        ways = [(1, (y + NY - d) % NY, up), (-1, (y + d) % NY, down)]
        if d == 4:
            ways = ways[:1]
        for way, yy, dev in ways:
            wait(s["w"].at[0], s["s_w"].at[hh * NY + yy])
            src = s["w"].at[at(hh, yy)]
            if d < 3 or (d == 3 and (k < 2) == (way == 1)):
                wsend(src, hh, yy, dev)
            cross(src, hh, yy)

    def experts(k):
        hh = (h + k) % NH
        wait(s["w"].at[pl.ds(0, NY)], s["s_cross"].at[hh])
        block = pl.ds(16 * hh, 16)
        cols = pl.ds(pl.multiple_of(512 * hh, 512), 512)
        xr, w = s["xr"], s["w"]

        def stacked(first, columns):
            lead = xr[:, first : first + 16, columns].reshape(128, -1)
            tail = xr[:, 32:48, columns].reshape(128, -1)
            return jnp.concatenate([lead, tail], axis=0)

        rows_in = stacked(0, cols)
        gate = dot_nn(rows_in, w[block, 0:32, :].reshape(512, FF))
        upper = dot_nn(rows_in, w[block, 32:64, :].reshape(512, FF))
        if k == 0:
            s["pre"][:, 0:FF] = gate
            s["pre"][:, FF : 2 * FF] = upper
        else:
            s["pre"][:, 0:FF] += gate
            s["pre"][:, FF : 2 * FF] += upper
        d0 = w[block, 64:80, :].reshape(256, FF)
        d1 = w[block, 80:96, :].reshape(256, FF)
        h0 = dot_nt(stacked(16, slice(0, 768)), d0) + dot_nt(stacked(16, slice(768, 1536)), d1)
        last = stacked(16, slice(1536, 2048))
        h1 = dot_nt(last, d0[:, 0:512])
        h2 = dot_nt(last[:, 0:256], d0[:, 512:768]) + dot_nt(last[:, 256:512], d1[:, 0:256])
        h3 = dot_nt(last, d1[:, 256:768])
        m = lax.broadcasted_iota(jnp.int32, (256, 256), 1) % 16
        z1 = jnp.where(m < 12, h0, h1)
        z2 = jnp.where(m < 12, pltpu.roll(h3, 252, 1), h2)
        hid = dot_nn(z1.astype(BF), s["sel"][k, 0]) + dot_nn(z2.astype(BF), s["sel"][k, 1])
        if k == 0:
            s["hid"][...] = hid
        else:
            s["hid"][...] += hid

    work = [
        [lambda: selection(0), lambda: selection(1)],
        [lambda: selection(2), lambda: selection(3)],
        [op_pass, halo_ready, lambda: forward(0)],
        [lambda: forward(1)],
        [lambda: op_cross(1, l), lambda: forward(2)],
        [lambda: forward(3)],
        [lambda: op_cross(2, 1 - l)],
    ]
    for d in range(0, 4):
        for k in range(NH):
            arrive(d, k)
            if d > 0 and work:
                for piece in work.pop(0):
                    piece()
    local[0].wait()
    own_x.wait()
    wait(s["xr"].at[pl.ds(0, 7)], s["s_x"].at[1])
    for k in range(NH):
        arrive(4, k)
    for k in range(NH):
        experts(k)

    for part in range(6):
        if part < 4:
            rows = slice(32 * part, 32 * part + 32)
            gate = s["pre"][rows, 0:FF]
            upper = s["pre"][rows, FF : 2 * FF]
            hid = s["hid"][rows, :]
        else:
            rows = slice(128 + 64 * (part - 4), 192 + 64 * (part - 4))
            gate = s["pre"][rows, 0:FF].reshape(4, 16, FF)[:, 0:8].reshape(32, FF)
            upper = s["pre"][rows, FF : 2 * FF].reshape(4, 16, FF)[:, 0:8].reshape(32, FF)
            hid = s["hid"][rows, :].reshape(4, 16, FF)[:, 8:16].reshape(32, FF)
        sigm = jax.nn.sigmoid(gate)
        put = pl.ds(32 * part, 32)
        s["gg"][put, 0:FF] = (hid * upper * sigm * (1.0 + gate * (1.0 - sigm))).astype(BF)
        s["gg"][put, FF : 2 * FF] = (hid * gate * sigm).astype(BF)

    gg, os = s["gg"], s["os"]

    def slot_grad(n):
        block = pl.ds(8 * n, 8)
        return dot_nt(gg[:, 0:FF], s["w"][block, 0:32, :].reshape(256, FF)) + dot_nt(
            gg[:, FF : 2 * FF], s["w"][block, 32:64, :].reshape(256, FF)
        )

    own_o = []
    for buf in range(2):
        for sub in range(2):
            cols = pl.ds(256 * sub, 256)
            o0 = slot_grad(4 * buf + sub)
            o1 = slot_grad(4 * buf + 2 + sub)
            os[buf, :, 0:16, cols] = o0[0:128].astype(BF).reshape(N_EXP, 16, 256)
            os[buf, :, 16:32, cols] = o1[0:128].astype(BF).reshape(N_EXP, 16, 256)
            tail = jnp.concatenate(
                [o0[128:192].reshape(N_EXP, 8, 256), o1[128:192].reshape(N_EXP, 8, 256)], axis=1
            )
            os[buf, :, 32:48, cols] = tail.astype(BF)
        for dev in exps:
            send(os.at[buf, dev[1]], s["orr"].at[buf, me], s["s_o"].at[buf], s["s_o"].at[2 + buf], dev)
        copy = pltpu.make_async_copy(os.at[buf, me], s["orr"].at[buf, me], s["s_local"].at[5 + buf])
        copy.start()
        own_o.append(copy)

    for buf in range(2):
        own_o[buf].wait()
        wait(s["orr"].at[buf, pl.ds(0, 7)], s["s_o"].at[2 + buf])
        got = s["orr"][buf].reshape(N_EXP * SLOTS, 512)
        s["ng"][:, 1024 * buf : 1024 * buf + 512] = dot_nn(s["tin"][...], got)
        s["ng"][:, 1024 * buf + 512 : 1024 * buf + 1024] = dot_nn(s["tdy"][...], got)
    for r in range(0, TOK_DEV, 16):
        rows = pl.ds(r, 16)
        inverse = s["inv"][rows, :]
        scaled = s["ng"][rows, :] * gain_f
        feats = res[rows, :].astype(F32)
        mean = jnp.mean(scaled * feats, axis=1, keepdims=True)
        total = dy[rows, :].astype(F32) + inverse * scaled - feats * (inverse * inverse * inverse * mean)
        out_res[rows, :] = total.astype(BF)

    local[1].wait()
    wait(s["opf"].at[pl.ds(0, 7), pl.ds(0, 64)], s["s_op_r"].at[3])
    own_h = None
    for step in (2, 1, 3, 0):
        pair = (x + step) % 4
        proj = s["opf"][pl.ds(2 * pair, 2)].reshape(2 * VD, D)
        grads = dot_nt(out_res[...], proj).astype(BF)
        s["hs"][2 * pair] = grads[:, 0:VD]
        s["hs"][2 * pair + 1] = grads[:, VD : 2 * VD]
        for parity in (0, 1):
            if step:
                e = 2 * pair + parity
                send(s["hs"].at[e], s["hr"].at[me], s["s_h"].at[0], s["s_h"].at[1], (ctx, e))
        if not step:
            e = lmate[1]
            send(s["hs"].at[e], s["hr"].at[me], s["s_h"].at[0], s["s_h"].at[1], (ctx, e))
            own_h = pltpu.make_async_copy(s["hs"].at[me], s["hr"].at[me], s["s_local"].at[7])
            own_h.start()
    s["dk"][...] = jnp.zeros((REACH + TOK, QK), F32)
    s["dv"][...] = jnp.zeros((REACH + TOK, VD), F32)
    own_h.wait()
    wait(s["hr"].at[pl.ds(0, 7)], s["s_h"].at[1])

    for b in range(N_QB):
        rows, window = pl.ds(QB * b, QB), pl.ds(QB * b, WIN)
        grad = s["hr"][2 * b : 2 * b + 2].reshape(QB, VD)
        delta = jnp.sum(grad.astype(F32) * s["att"][rows, :], axis=1, keepdims=True)
        prob_grad = dot_nt(grad, s["vw"][window, :])
        score_grad = (s["probs"][b] * (prob_grad - delta)).astype(BF)
        s["dv"][window, :] += dot_nn(s["plt"][b], grad)
        s["dk"][window, :] += dot_tn(score_grad, q[rows, :])
        out_q[rows, :] = (dot_nn(score_grad, s["kw"][window, :]) * SCALE).astype(BF)
        if b == 1:
            s["ks"][...] = (s["dk"][0:REACH, :] * SCALE).astype(BF)
            s["vs"][...] = s["dv"][0:REACH, :].astype(BF)
            send(s["ks"], s["kr"], s["s_k"].at[0], s["s_k"].at[1], before)
            send(s["vs"], s["vr"], s["s_k"].at[2], s["s_k"].at[3], before)
    out_k[0:REACH, :] = (s["dk"][REACH : 2 * REACH, :] * SCALE).astype(BF)
    out_v[0:REACH, :] = s["dv"][REACH : 2 * REACH, :].astype(BF)
    wait(s["kr"], s["s_k"].at[1])
    out_k[REACH:TOK, :] = (
        s["dk"][2 * REACH : 3 * REACH, :] * SCALE + s["kr"][...].astype(F32)
    ).astype(BF)
    wait(s["vr"], s["s_k"].at[3])
    out_v[REACH:TOK, :] = (s["dv"][2 * REACH : 3 * REACH, :] + s["vr"][...].astype(F32)).astype(BF)

    wait(s["w"].at[pl.ds(0, 63)], s["s_wsend"])
    wait(s["opf"].at[pl.ds(0, 7)], s["s_op_s"])
    wait(keys_in.at[pl.ds(0, REACH)], s["s_halo_s"].at[0])
    wait(values_in.at[pl.ds(0, REACH)], s["s_halo_s"].at[1])
    wait(s["segh"], s["s_halo_s"].at[2])
    wait(s["xs"].at[pl.ds(0, 7)], s["s_x"].at[0])
    for buf in range(2):
        wait(os.at[buf, pl.ds(0, 7)], s["s_o"].at[buf])
    wait(s["hs"].at[pl.ds(0, 7)], s["s_h"].at[0])
    wait(s["ks"], s["s_k"].at[0])
    wait(s["vs"], s["s_k"].at[2])


def shards(
    residual, out_grad, norm_gain, expert_ids, route_weights, gate_up, down_proj, out_proj,
    queries, keys_in, values_in, segments,
):
    down = down_proj.reshape(12, D)
    packed = jnp.concatenate([down[:, :1536], down[:, 1536:].reshape(4, 1536)], axis=0)
    share = jnp.concatenate([gate_up.reshape(64, FF), packed[:, :FF], packed[:, FF:]], axis=0)
    vm = pl.BlockSpec(memory_space=pltpu.VMEM)
    hbm = pl.BlockSpec(memory_space=pl.ANY)
    return pl.pallas_call(
        body,
        out_shape=(
            jax.ShapeDtypeStruct((TOK_DEV, D), BF),
            jax.ShapeDtypeStruct((TOK, QK), BF),
            jax.ShapeDtypeStruct((TOK, QK), BF),
            jax.ShapeDtypeStruct((TOK, VD), BF),
        ),
        in_specs=[hbm] * 4 + [vm] * 7,
        out_specs=(vm,) * 4,
        scratch_shapes=list(scratch().values()),
        compiler_params=pltpu.CompilerParams(
            collective_id=0, has_side_effects=True, vmem_limit_bytes=60 * 1024 * 1024
        ),
    )(
        share, out_proj, keys_in, values_in, residual, out_grad, norm_gain.reshape(1, D),
        expert_ids, route_weights, segments.reshape(8, 128), queries,
    )


def solution(mesh):
    return jax.shard_map(
        shards,
        mesh=mesh,
        in_specs=(
            P(("ctx", "exp"), None),
            P(("ctx", "exp"), None),
            P(),
            P(("ctx", "exp"), None),
            P(("ctx", "exp"), None),
            P("exp", None, "ctx", None),
            P("exp", "ctx", None),
            P("exp", None),
            P("ctx", "exp"),
            P("ctx", "exp"),
            P("ctx", "exp"),
            P("ctx"),
        ),
        out_specs=(P(("ctx", "exp"), None), P("ctx", "exp"), P("ctx", "exp"), P("ctx", "exp")),
        check_vma=False,
    )
```

time: 361 us -> 127 us (0.35)
  waiting for transfers between devices: 246 us -> 0 us
  Pallas kernels: 0 us -> 112 us
  matrix products: 36.1 us -> 0 us
  starting transfers between devices: 30.6 us -> 0 us
  blocking collectives: 16 us -> 0 us
  between operations: 14.1 us -> 0.68 us
  other arithmetic: 7.12 us -> 1.59 us
    all_gather x3 -> x0, waiting for transfers between devices: 226 us -> none  [the longest x1 88.3 us: expert_rows(): lax.all_gather(gate_up, 'ctx', axis=2, tiled=True)]
    pallas_call x0 -> x1, Pallas kernels: none -> 112 us  [shards(): pl.pallas_call(body, out_shape=(jax.ShapeDtypeStruct((TOK_DEV, D), BF), j...]
    dot_general x14 -> x0, matrix products: 36.1 us -> none  [the longest x4 19.6 us: contract_last(): lax.dot_general(left, right, (((1,), (1,)), ((), ())), preferred_element_...]
    ppermute x5 -> x0, starting transfers between devices: 17.5 us -> none  [shifted(): return lax.ppermute(value, axis, pairs)]
    all_to_all x1 -> x0, blocking collectives: 16 us -> none  [shards(): lax.all_to_all(slot_out.reshape(n_exp, capacity, D), 'exp', split_axis=0,...]
    all_to_all x3 -> x0, starting transfers between devices: 12.9 us -> none  [the longest x1 5.83 us: shards(): lax.all_to_all(slot_gate.reshape(n_exp, capacity), 'exp', split_axis=0, c...]
    all_to_all x3 -> x0, waiting for transfers between devices: 9.96 us -> none  [the longest x1 7.6 us: shards(): lax.all_to_all(slot_dy.reshape(n_exp, capacity, D), 'exp', split_axis=0,...]
    ppermute x5 -> x0, waiting for transfers between devices: 9.43 us -> none  [shifted(): return lax.ppermute(value, axis, pairs)]
  transfers between devices with their start and end apart: 11 -> 0, of which waited for: 8 -> 0; matrix products, arithmetic and copies ran while one was open for 6% -> 0% of each run, Pallas kernels for 0% -> 0%
where the time goes in v1:
time: 127 us; the launch traced here: 126 us
  Pallas kernels  112 us (88%)
  local copies, waits for them, and re-layouts  11.9 us (9%)
  other arithmetic  1.59 us (1%)
    pallas_call x1, Pallas kernels, shards(): pl.pallas_call(body, out_shape=(jax.ShapeDtypeStruct((TOK_DEV, D), BF), j...  112 us
    unnamed x18, local copies, waits for them, and re-layouts  6.06 us
    pallas_call x2, local copies, waits for them, and re-layouts, shards(): pl.pallas_call(body, out_shape=(jax.ShapeDtypeStruct((TOK_DEV, D), BF), j...  2.97 us

profile of v1, /device:TPU:57, one launch (start us, length us, event | category | flops | bytes accessed | tf_op | source)
XLA Modules:
  0.0 126.1 jit_solution(11433979812445020724)
XLA Ops:
  0.6 0.0 copy-start.2
  0.6 1.3 %reshape.26.gain = bf16[1,2048]{1,0:T(2,128)(2,1)} reshape(bf16[2048]{0:T(1024)(128)(2,1)} %param.14) | data formatting | bytes 8192 | tf_op jit(solution)/shard_map/reshape | solution.py:479
  2.0 0.7 slice.17
  2.7 1.4 %copy.18.rw = bf16[128,6]{1,0:T(8,128)(2,1)} copy(bf16[128,6]{0,1:T(8,128)(2,1)} %param.16) | data formatting | bytes 3072 | tf_op args[4]
  4.1 0.8 slice.16
  5.0 0.0 copy-start.5
  5.0 1.6 %fusion.w_in = bf16[96,768]{1,0:T(8,128)(2,1)} fusion(bf16[4,1536]{1,0:T(4,128)(2,1)S(1)} %reshape.25, bf16[12,1536]{1,0:T(8,128)(2,1)S(1)} %slice.16, bf16[16,768]{1,0:T(8,128)(2,1)S(1)} %fusion.1, bf16[64,768]{1,0:T(8,128)(2,1)} %bitcast.3), kind=kLoop, calls=%fused_computation.1 | loop fusion | flops 589824 | bytes 319488 | tf_op jit(solution)/shard_map/concatenate | solution.py:461
  6.5 0.0 copy-done.5
  6.5 0.7 copy.17.ids
  7.3 0.0 copy-done.2
  7.3 0.0 copy-start.3
  7.3 1.0 copy.19.q
  8.3 0.0 copy-done.3
  8.3 1.0 copy.16.keys_in
  9.3 111.9 %shard_map.147 = (bf16[128,2048]{1,0:T(8,128)(2,1)}, bf16[1024,192]{1,0:T(8,128)(2,1)}, bf16[1024,192]{1,0:T(8,128)(2,1)}, bf16[1024,128]{1,0:T(8,128)(2,1)}) custom-call(bf16[96,768]{1,0:T(8,128)(2,1)} %fusion.w_in, bf16[128,2048]{1,0:T(8,128)(2,1)} %op_in.1, bf16[1024,192]{1,0:T(8,128)(2,1)} %copy.16.keys_in, bf16[1024,128]{1,0:T(8,128)(2,1)} %values_in.1, ...), custom_call_target="tpu_custom_call" | custom-call | tf_op jit(solution)/shard_map/pallas_call | solution.py:464
  121.2 0.0 copy-start
  121.3 2.0 %copy.20 = bf16[1024,192]{0,1:T(8,128)(2,1)} copy(bf16[1024,192]{1,0:T(8,128)(2,1)} %get-tuple-element.5) | data formatting | bytes 786432 | tf_op jit(solution)/shard_map/pallas_call | solution.py:464
  123.3 0.0 copy-done
  123.3 0.0 copy-start.1
  123.3 0.9 copy.21
  124.2 0.1 copy-done.1
  124.3 0.8 copy.24
  125.1 0.3 copy-done.4
  125.4 0.7 copy.25
  (3 shorter events, 0.0 us)
Async XLA Ops:
  0.6 6.7 %copy-start.2 = (bf16[1024,192]{0,1:T(8,128)(2,1)S(1)}, bf16[1024,192]{0,1:T(8,128)(2,1)}, u32[]{:S(2)}) copy-start(bf16[1024,192]{0,1:T(8,128)(2,1)} %param.20) | copy-start | bytes 1179652
  5.0 1.6 %copy-start.5 = (s32[128,6]{0,1:T(8,128)S(1)}, s32[128,6]{0,1:T(8,128)}, u32[]{:S(2)}) copy-start(s32[128,6]{0,1:T(8,128)} %param.15) | copy-start | bytes 9220
  7.3 1.0 copy-start.3
  121.2 2.0 %copy-start = (bf16[1024,192]{1,0:T(8,128)(2,1)S(1)}, bf16[1024,192]{1,0:T(8,128)(2,1)}, u32[]{:S(2)}) copy-start(bf16[1024,192]{1,0:T(8,128)(2,1)} %get-tuple-element.6) | copy-start | bytes 1179652
  123.3 1.0 copy-start.1
  124.3 1.1 copy-start.4

commit v2 on v1

--- a/solution.py
+++ b/solution.py
@@ -21,6 +21,7 @@
 TOK_DEV = 128
 CAP = 24
 SLOTS = 48
+LIVE = N_EXP * CAP
 SHARD = 96
 QB = 256
 WIN = QB + REACH
@@ -56,28 +57,35 @@
         sel=vm((NH, 2, 256, FF), BF),
         pre=vm((256, 2 * FF), F32),
         hid=vm((256, FF), F32),
-        gg=vm((192, 2 * FF), BF),
+        gg=vm((LIVE, 2 * FF), BF),
         os=vm((2, N_EXP, SLOTS, 512), BF),
         orr=vm((2, N_EXP, SLOTS, 512), BF),
         tin=vm((TOK_DEV, N_EXP * SLOTS), BF),
         tdy=vm((TOK_DEV, N_EXP * SLOTS), BF),
         inv=vm((TOK_DEV, 1), F32),
-        ng=vm((TOK_DEV, D), F32),
-        hs=vm((N_EXP, TOK_DEV, VD), BF),
-        hr=vm((N_EXP, TOK_DEV, VD), BF),
-        kw=vm((REACH + TOK, QK), BF),
+        auxs=vm((N_EXP, CAP, 128), F32),
+        auxr=vm((N_EXP, CAP, 128), F32),
+        places=vm((8, 128), jnp.int32),
+        placer=vm((N_EXP, 8, 128), jnp.int32),
+        tab=vm((N_EXP, TOK_DEV, 256), BF),
+        ng=vm((LIVE, D), F32),
+        rg=vm((LIVE, D), BF),
+        hs=vm((N_EXP, LIVE, VD), BF),
+        hr=vm((N_EXP, LIVE, VD), BF),
+        grads=vm((TOK, VD), BF),
+        kw=vm((QK, REACH + TOK), BF),
         vw=vm((REACH + TOK, VD), BF),
         segh=vm((8, 128), jnp.int32),
         probs=vm((N_QB, QB, WIN), F32),
         plt=vm((N_QB, WIN, QB), BF),
         att=vm((TOK, VD), F32),
-        dk=vm((REACH + TOK, QK), F32),
+        dk=vm((QK, REACH + TOK), F32),
         dv=vm((REACH + TOK, VD), F32),
-        ks=vm((REACH, QK), BF),
+        ks=vm((QK, REACH), BF),
         vs=vm((REACH, VD), BF),
-        kr=vm((REACH, QK), BF),
+        kr=vm((QK, REACH), BF),
         vr=vm((REACH, VD), BF),
-        s_local=dma((8,)),
+        s_local=dma((10,)),
         s_wsend=dma,
         s_w=dma((NH * NY,)),
         s_cross=dma((NH,)),
@@ -86,6 +94,7 @@
         s_op_s=dma,
         s_op_r=dma((4,)),
         s_x=dma((2,)),
+        s_aux=dma((4,)),
         s_o=dma((4,)),
         s_h=dma((2,)),
         s_k=dma((4,)),
@@ -96,7 +105,7 @@
 
 
 def body(
-    w_in, op_in, keys_in, values_in, res, dy, gain, ids, rw, seg, q,
+    gu_in, op_in, keys_in, values_in, down_in, res, dy, gain, ids, rw, seg, qt,
     out_res, out_q, out_k, out_v, *rest,
 ):
     s = dict(zip(NAMES, rest))
@@ -131,13 +140,23 @@
     for dev in partners:
         pl.semaphore_signal(barrier, inc=1, device_id=dev, device_id_type=MESH)
     local = [
-        pltpu.make_async_copy(w_in, s["w"].at[ctx], s["s_local"].at[0]),
+        pltpu.make_async_copy(gu_in, s["w"].at[ctx, pl.ds(0, 64)], s["s_local"].at[0]),
         pltpu.make_async_copy(op_in, s["opf"].at[me], s["s_local"].at[1]),
-        pltpu.make_async_copy(keys_in, s["kw"].at[pl.ds(REACH, TOK)], s["s_local"].at[2]),
+        pltpu.make_async_copy(keys_in, s["kw"].at[:, pl.ds(REACH, TOK)], s["s_local"].at[2]),
         pltpu.make_async_copy(values_in, s["vw"].at[pl.ds(REACH, TOK)], s["s_local"].at[3]),
     ]
     for copy in local:
         copy.start()
+    rows12 = down_in[...].astype(F32)
+    tail = [
+        jnp.concatenate([rows12[3 * a + b : 3 * a + b + 1, 1536:2048] for a in range(4)], axis=0)
+        for b in range(3)
+    ]
+    rows16 = jnp.concatenate([rows12[:, 0:1536], jnp.concatenate(tail, axis=1)], axis=0).astype(BF)
+    s["w"][ctx, 64:80, :] = rows16[:, 0:768]
+    s["w"][ctx, 80:96, :] = rows16[:, 768:1536]
+    local[0].wait()
+    w_in = s["w"].at[ctx]
     pl.semaphore_wait(barrier, len(partners))
 
     def wsend(src, hh, yy, dev):
@@ -154,50 +173,95 @@
     cross(w_in, h, y)
     half = pl.ds(64 * c, 64)
     send(op_in.at[half], s["opf"].at[me, half], s["s_op_s"], s["s_op_r"].at[0], lmate)
-    send(keys_in.at[pl.ds(REACH, REACH)], s["kw"].at[pl.ds(0, REACH)],
+    for dev in xmates:
+        send(op_in.at[half], s["opf"].at[me, half], s["s_op_s"], s["s_op_r"].at[1], dev)
+    send(keys_in.at[:, pl.ds(REACH, REACH)], s["kw"].at[:, pl.ds(0, REACH)],
          s["s_halo_s"].at[0], s["s_halo_r"].at[0], after)
     send(values_in.at[pl.ds(REACH, REACH)], s["vw"].at[pl.ds(0, REACH)],
          s["s_halo_s"].at[1], s["s_halo_r"].at[1], after)
     send(seg, s["segh"], s["s_halo_s"].at[2], s["s_halo_r"].at[2], after)
 
-    gain_f = gain[...].astype(F32)
-    for r in range(0, TOK_DEV, 16):
-        rows = pl.ds(r, 16)
-        feats = res[rows, :].astype(F32)
-        inverse = lax.rsqrt(jnp.mean(feats * feats, axis=1, keepdims=True) + EPSILON)
-        s["inv"][rows, :] = inverse
-        s["lhs"][rows, :] = (feats * inverse * gain_f).astype(BF)
-    s["lhs"][pl.ds(TOK_DEV, TOK_DEV), :] = dy[...]
+    gain_rows = gain[...].astype(F32)
+    gain_f = jnp.concatenate([gain_rows[i : i + 1, :] for i in range(16)], axis=1)
+
+    def normalize():
+        for r in range(0, TOK_DEV, 16):
+            rows = pl.ds(r, 16)
+            feats = res[rows, :].astype(F32)
+            inverse = lax.rsqrt(jnp.mean(feats * feats, axis=1, keepdims=True) + EPSILON)
+            s["inv"][rows, :] = inverse
+            s["lhs"][rows, :] = (feats * inverse * gain_f).astype(BF)
+        s["lhs"][pl.ds(TOK_DEV, TOK_DEV), :] = dy[...]
 
     ids_v = ids[...]
     live = ids_v < N_EXP
-    expert = jnp.sum(jnp.where(live, ids_v, 0), axis=1, keepdims=True)
-    weight = jnp.sum(jnp.where(live, rw[...].astype(F32), 0.0), axis=1, keepdims=True)
-    lane = lax.broadcasted_iota(jnp.int32, (TOK_DEV, 128), 1)
-    row = lax.broadcasted_iota(jnp.int32, (TOK_DEV, 128), 0)
-    onehot = jnp.where(lane == expert, 1.0, 0.0)
-    earlier = jnp.where(lane < row, 1.0, 0.0).astype(BF)
-    counts = dot_nn(earlier, onehot.astype(BF))
-    rank = jnp.sum(onehot * counts, axis=1, keepdims=True).astype(jnp.int32)
+    expert = jnp.sum(jnp.where(live, ids_v, 0), axis=0, keepdims=True)
+    first = lax.broadcasted_iota(jnp.int32, (TOK_DEV, TOK_DEV), 0)
+    second = lax.broadcasted_iota(jnp.int32, (TOK_DEV, TOK_DEV), 1)
+    earlier = jnp.where(first < second, 1.0, 0.0).astype(BF)
+    onehot = jnp.where(lax.broadcasted_iota(jnp.int32, (16, TOK_DEV), 0) == expert, 1.0, 0.0)
+    counts = dot_nn(onehot.astype(BF), earlier)
+    rank = jnp.sum(onehot * counts, axis=0, keepdims=True).astype(jnp.int32)
     place_in = expert * SLOTS + jnp.where(rank < 16, rank, rank + 16)
     place_dy = expert * SLOTS + jnp.where(rank < 16, rank + 16, rank + 24)
-    slot = lax.broadcasted_iota(jnp.int32, (TOK_DEV, N_EXP * SLOTS), 1)
-    hit_in = slot == place_in
-    hit_dy = slot == place_dy
-    s["tin"][...] = jnp.where(hit_in, weight, 0.0).astype(BF)
-    s["tdy"][...] = jnp.where(hit_dy, weight, 0.0).astype(BF)
-    table = jnp.concatenate(
-        [jnp.where(hit_in, 1.0, 0.0).astype(BF), jnp.where(hit_dy, 1.0, 0.0).astype(BF)], axis=0
-    )
-    for col in range(0, D, 512):
-        picked = dot_tn(table, s["lhs"][:, col : col + 512])
-        s["xs"][:, :, col : col + 512] = picked.astype(BF).reshape(N_EXP, SLOTS, 512)
-    for dev in exps:
-        send(s["xs"].at[dev[1]], s["xr"].at[me], s["s_x"].at[0], s["s_x"].at[1], dev)
-    own_x = pltpu.make_async_copy(s["xs"].at[me], s["xr"].at[me], s["s_local"].at[4])
-    own_x.start()
-    for dev in xmates:
-        send(op_in.at[half], s["opf"].at[me, half], s["s_op_s"], s["s_op_r"].at[1], dev)
+    slot = lax.broadcasted_iota(jnp.int32, (N_EXP * SLOTS, TOK_DEV), 0)
+    hit_in = jnp.where(slot == place_in, 1.0, 0.0).astype(BF)
+    hit_dy = jnp.where(slot == place_dy, 1.0, 0.0).astype(BF)
+
+    def dispatch(*columns):
+        table = jnp.concatenate([hit_in, hit_dy], axis=1)
+        for col in columns:
+            picked = dot_nn(table, s["lhs"][:, col : col + 512])
+            s["xs"][:, :, col : col + 512] = picked.astype(BF).reshape(N_EXP, SLOTS, 512)
+
+    own = [
+        pltpu.make_async_copy(s["xs"].at[me], s["xr"].at[me], s["s_local"].at[4]),
+        pltpu.make_async_copy(s["auxs"].at[me], s["auxr"].at[me], s["s_local"].at[8]),
+        pltpu.make_async_copy(s["places"], s["placer"].at[me], s["s_local"].at[9]),
+    ]
+
+    def dispatch_send():
+        for dev in exps:
+            send(s["xs"].at[dev[1]], s["xr"].at[me], s["s_x"].at[0], s["s_x"].at[1], dev)
+        own[0].start()
+
+    def side_send():
+        weight = jnp.sum(jnp.where(live, rw[...].astype(F32), 0.0), axis=0, keepdims=True)
+        weight = jnp.transpose(jnp.broadcast_to(weight, (8, TOK_DEV)))[:, 0:1]
+        inverse = s["inv"][...]
+        high = inverse.astype(BF).astype(F32)
+        mid = (inverse - high).astype(BF).astype(F32)
+        low = inverse - high - mid
+        lane = lax.broadcasted_iota(jnp.int32, (TOK_DEV, 128), 1)
+        terms = jnp.where(lane == 0, high, jnp.where(lane == 1, mid, jnp.where(lane == 2, low, jnp.where(lane == 3, weight, 0.0))))
+        picked = dot_nn(hit_in, terms.astype(BF)).reshape(N_EXP, SLOTS, 128)
+        s["auxs"][:, 0:16, :] = picked[:, 0:16]
+        s["auxs"][:, 16:24, :] = picked[:, 32:40]
+        code = expert * 16 + jnp.where(rank < 16, rank, rank + 112 + 8 * (me % 2))
+        s["places"][...] = jnp.broadcast_to(code, (8, 128))
+        for dev in exps:
+            send(s["auxs"].at[dev[1]], s["auxr"].at[me], s["s_aux"].at[0], s["s_aux"].at[1], dev)
+            send(s["places"], s["placer"].at[me], s["s_aux"].at[2], s["s_aux"].at[3], dev)
+        own[1].start()
+        own[2].start()
+
+    def tables():
+        s["tin"][...] = jnp.transpose(hit_in)
+        s["tdy"][...] = jnp.transpose(hit_dy)
+
+    def places_ready():
+        own[2].wait()
+        wait(s["placer"].at[pl.ds(0, 7)], s["s_aux"].at[3])
+
+    def place_table(src):
+        at_row = lax.broadcasted_iota(jnp.int32, (256, TOK_DEV), 0) == s["placer"][src, 0:1, :]
+        s["tab"][src] = jnp.transpose(jnp.where(at_row, 1.0, 0.0).astype(BF))
+
+    def rows_ready():
+        own[0].wait()
+        own[1].wait()
+        wait(s["xr"].at[pl.ds(0, 7)], s["s_x"].at[1])
+        wait(s["auxr"].at[pl.ds(0, 7)], s["s_aux"].at[1])
 
     def selection(k):
         hh = (h + k) % NH
@@ -211,7 +275,7 @@
         s["sel"][k, 1] = jnp.where(f == second, 1.0, 0.0).astype(BF)
 
     def halo_ready():
-        wait(s["kw"].at[pl.ds(0, REACH)], s["s_halo_r"].at[0])
+        wait(s["kw"].at[:, pl.ds(0, REACH)], s["s_halo_r"].at[0])
         wait(s["vw"].at[pl.ds(0, REACH)], s["s_halo_r"].at[1])
         wait(s["segh"], s["s_halo_r"].at[2])
         local[2].wait()
@@ -225,7 +289,7 @@
         seg_q = jnp.concatenate([seg_cols[:, 2 * b : 2 * b + 1], seg_cols[:, 2 * b + 1 : 2 * b + 2]], axis=0)
         pos_q = lax.broadcasted_iota(jnp.int32, (QB, 128), 0) + REACH
         pos_k = lax.broadcasted_iota(jnp.int32, (QB, 128), 1)
-        scores = dot_nt(q[pl.ds(QB * b, QB), :], s["kw"][pl.ds(QB * b, WIN), :]) * SCALE
+        scores = dot_nn(jnp.transpose(qt[:, pl.ds(QB * b, QB)]), s["kw"][:, pl.ds(QB * b, WIN)]) * SCALE
         pieces = []
         for t in range(WIN // 128):
             allowed = (seg_q == seg_row(2 * b + t)) & (pos_k + 128 * t <= pos_q)
@@ -256,24 +320,17 @@
             e = 2 * ((x + step) % 4) + parity
             send(s["opf"].at[e, half], s["opf"].at[e, half], s["s_op_s"], s["s_op_r"].at[3], sibling)
 
-    def arrive(d, k):
+    def arrive(d, k, way):
         hh = (h + k) % NH
-        if d == 0:
-            if k > 0:
-                wait(s["w"].at[0], s["s_w"].at[hh * NY + y])
-                src = s["w"].at[at(hh, y)]
-                wsend(src, hh, y, up)
-                wsend(src, hh, y, down)
-                cross(src, hh, y)
-            return
-        ways = [(1, (y + NY - d) % NY, up), (-1, (y + d) % NY, down)]
-        if d == 4:
-            ways = ways[:1]
-        for way, yy, dev in ways:
+        yy = (y + NY - way * d) % NY
+        if d + k > 0:
             wait(s["w"].at[0], s["s_w"].at[hh * NY + yy])
             src = s["w"].at[at(hh, yy)]
-            if d < 3 or (d == 3 and (k < 2) == (way == 1)):
-                wsend(src, hh, yy, dev)
+            if d == 0:
+                wsend(src, hh, yy, up)
+                wsend(src, hh, yy, down)
+            elif d < 3 or (d == 3 and (k < 2) == (way == 1)):
+                wsend(src, hh, yy, up if way == 1 else down)
             cross(src, hh, yy)
 
     def experts(k):
@@ -313,28 +370,44 @@
         else:
             s["hid"][...] += hid
 
-    work = [
-        [lambda: selection(0), lambda: selection(1)],
-        [lambda: selection(2), lambda: selection(3)],
-        [op_pass, halo_ready, lambda: forward(0)],
-        [lambda: forward(1)],
-        [lambda: op_cross(1, l), lambda: forward(2)],
-        [lambda: forward(3)],
-        [lambda: op_cross(2, 1 - l)],
+    normalize()
+    steps = [
+        (1, 0, -1), (1, 0, 1),
+        lambda: dispatch(0, 512),
+        (0, 1, 0), (0, 3, 0),
+        lambda: dispatch(1024, 1536), dispatch_send,
+        (2, 0, -1), (2, 0, 1),
+        side_send,
+        (1, 1, -1), (1, 1, 1), (0, 2, 0),
+        tables, lambda: selection(0),
+        (1, 3, -1), (1, 3, 1),
+        lambda: selection(1), op_pass,
+        (3, 0, -1), (3, 0, 1),
+        halo_ready, lambda: forward(0),
+        (2, 1, -1), (2, 1, 1),
+        lambda: forward(1),
+        (1, 2, -1), (1, 2, 1),
+        lambda: forward(2), lambda: op_cross(1, l),
+        (2, 3, -1), (2, 3, 1),
+        lambda: forward(3),
+        (3, 1, -1), (4, 0, 1),
+        places_ready, lambda: [place_table(src) for src in range(4)],
+        (2, 2, -1), (3, 1, 1),
+        lambda: [place_table(src) for src in range(4, 8)], lambda: selection(2),
+        (2, 2, 1), (3, 3, -1),
+        lambda: selection(3), rows_ready, lambda: experts(0),
+        (3, 2, -1), (3, 3, 1),
+        lambda: op_cross(2, 1 - l),
+        (4, 1, 1), (4, 3, -1),
+        lambda: experts(1),
+        (3, 2, 1), (4, 2, -1),
+        lambda: experts(3), lambda: experts(2),
     ]
-    for d in range(0, 4):
-        for k in range(NH):
-            arrive(d, k)
-            if d > 0 and work:
-                for piece in work.pop(0):
-                    piece()
-    local[0].wait()
-    own_x.wait()
-    wait(s["xr"].at[pl.ds(0, 7)], s["s_x"].at[1])
-    for k in range(NH):
-        arrive(4, k)
-    for k in range(NH):
-        experts(k)
+    for step in steps:
+        if callable(step):
+            step()
+        else:
+            arrive(*step)
 
     for part in range(6):
         if part < 4:
@@ -353,45 +426,53 @@
         s["gg"][put, FF : 2 * FF] = (hid * gate * sigm).astype(BF)
 
     gg, os = s["gg"], s["os"]
-
-    def slot_grad(n):
-        block = pl.ds(8 * n, 8)
-        return dot_nt(gg[:, 0:FF], s["w"][block, 0:32, :].reshape(256, FF)) + dot_nt(
-            gg[:, FF : 2 * FF], s["w"][block, 32:64, :].reshape(256, FF)
+    xr = s["xr"]
+    side = jnp.concatenate(
+        [s["auxr"][:, 0:16, :].reshape(128, 128), s["auxr"][:, 16:24, :].reshape(64, 128)], axis=0
+    )
+    inverse = side[:, 0:1] + side[:, 1:2] + side[:, 2:3]
+    weight = side[:, 3:4]
+
+    def slot_rows(first, cols):
+        lead = xr[:, 16 * first : 16 * first + 16, cols].reshape(128, -1).astype(F32)
+        tail = xr[:, 32:48, cols].astype(F32)[:, 8 * first : 8 * first + 8].reshape(64, -1)
+        return jnp.concatenate([lead, tail], axis=0)
+
+    dots = jnp.zeros((LIVE, 128), F32)
+    for n in range(8):
+        block, cols = pl.ds(8 * n, 8), pl.ds(256 * n, 256)
+        grad = weight * (
+            dot_nt(gg[:, 0:FF], s["w"][block, 0:32, :].reshape(256, FF))
+            + dot_nt(gg[:, FF : 2 * FF], s["w"][block, 32:64, :].reshape(256, FF))
         )
-
-    own_o = []
+        s["ng"][:, cols] = grad
+        prod = grad * slot_rows(0, cols)
+        dots = dots + prod[:, 0:128] + prod[:, 128:256]
+    share = inverse * (jnp.sum(dots, axis=1, keepdims=True) / D)
+    gain_inv = 1.0 / gain_f
+
+    def total(n):
+        cols = pl.ds(256 * n, 256)
+        lanes = slice(256 * n, 256 * n + 256)
+        value = (
+            slot_rows(1, cols)
+            + inverse * (s["ng"][:, cols] * gain_f[:, lanes])
+            - slot_rows(0, cols) * share * gain_inv[:, lanes]
+        )
+        s["rg"][:, cols] = value.astype(BF)
+        return value
+
     for buf in range(2):
         for sub in range(2):
             cols = pl.ds(256 * sub, 256)
-            o0 = slot_grad(4 * buf + sub)
-            o1 = slot_grad(4 * buf + 2 + sub)
+            o0 = total(4 * buf + sub)
+            o1 = total(4 * buf + 2 + sub)
             os[buf, :, 0:16, cols] = o0[0:128].astype(BF).reshape(N_EXP, 16, 256)
             os[buf, :, 16:32, cols] = o1[0:128].astype(BF).reshape(N_EXP, 16, 256)
             tail = jnp.concatenate(
                 [o0[128:192].reshape(N_EXP, 8, 256), o1[128:192].reshape(N_EXP, 8, 256)], axis=1
             )
             os[buf, :, 32:48, cols] = tail.astype(BF)
-        for dev in exps:
-            send(os.at[buf, dev[1]], s["orr"].at[buf, me], s["s_o"].at[buf], s["s_o"].at[2 + buf], dev)
-        copy = pltpu.make_async_copy(os.at[buf, me], s["orr"].at[buf, me], s["s_local"].at[5 + buf])
-        copy.start()
-        own_o.append(copy)
-
-    for buf in range(2):
-        own_o[buf].wait()
-        wait(s["orr"].at[buf, pl.ds(0, 7)], s["s_o"].at[2 + buf])
-        got = s["orr"][buf].reshape(N_EXP * SLOTS, 512)
-        s["ng"][:, 1024 * buf : 1024 * buf + 512] = dot_nn(s["tin"][...], got)
-        s["ng"][:, 1024 * buf + 512 : 1024 * buf + 1024] = dot_nn(s["tdy"][...], got)
-    for r in range(0, TOK_DEV, 16):
-        rows = pl.ds(r, 16)
-        inverse = s["inv"][rows, :]
-        scaled = s["ng"][rows, :] * gain_f
-        feats = res[rows, :].astype(F32)
-        mean = jnp.mean(scaled * feats, axis=1, keepdims=True)
-        total = dy[rows, :].astype(F32) + inverse * scaled - feats * (inverse * inverse * inverse * mean)
-        out_res[rows, :] = total.astype(BF)
 
     local[1].wait()
     wait(s["opf"].at[pl.ds(0, 7), pl.ds(0, 64)], s["s_op_r"].at[3])
@@ -399,7 +480,7 @@
     for step in (2, 1, 3, 0):
         pair = (x + step) % 4
         proj = s["opf"][pl.ds(2 * pair, 2)].reshape(2 * VD, D)
-        grads = dot_nt(out_res[...], proj).astype(BF)
+        grads = dot_nt(s["rg"][...], proj).astype(BF)
         s["hs"][2 * pair] = grads[:, 0:VD]
         s["hs"][2 * pair + 1] = grads[:, VD : 2 * VD]
         for parity in (0, 1):
@@ -411,40 +492,63 @@
             send(s["hs"].at[e], s["hr"].at[me], s["s_h"].at[0], s["s_h"].at[1], (ctx, e))
             own_h = pltpu.make_async_copy(s["hs"].at[me], s["hr"].at[me], s["s_local"].at[7])
             own_h.start()
-    s["dk"][...] = jnp.zeros((REACH + TOK, QK), F32)
+
+    own_o = []
+    for buf in range(2):
+        for dev in exps:
+            send(os.at[buf, dev[1]], s["orr"].at[buf, me], s["s_o"].at[buf], s["s_o"].at[2 + buf], dev)
+        copy = pltpu.make_async_copy(os.at[buf, me], s["orr"].at[buf, me], s["s_local"].at[5 + buf])
+        copy.start()
+        own_o.append(copy)
+    s["dk"][...] = jnp.zeros((QK, REACH + TOK), F32)
     s["dv"][...] = jnp.zeros((REACH + TOK, VD), F32)
     own_h.wait()
     wait(s["hr"].at[pl.ds(0, 7)], s["s_h"].at[1])
 
+    for src in range(N_EXP):
+        lead = s["hr"][:, 16 * src : 16 * src + 16, :].reshape(128, VD)
+        tail = s["hr"][:, 128 + 16 * (src // 2) : 144 + 16 * (src // 2), :].reshape(128, VD)
+        rows = dot_nn(s["tab"][src], jnp.concatenate([lead, tail], axis=0))
+        s["grads"][TOK_DEV * src : TOK_DEV * src + TOK_DEV, :] = rows.astype(BF)
+
     for b in range(N_QB):
         rows, window = pl.ds(QB * b, QB), pl.ds(QB * b, WIN)
-        grad = s["hr"][2 * b : 2 * b + 2].reshape(QB, VD)
+        grad = s["grads"][rows, :]
         delta = jnp.sum(grad.astype(F32) * s["att"][rows, :], axis=1, keepdims=True)
         prob_grad = dot_nt(grad, s["vw"][window, :])
         score_grad = (s["probs"][b] * (prob_grad - delta)).astype(BF)
         s["dv"][window, :] += dot_nn(s["plt"][b], grad)
-        s["dk"][window, :] += dot_tn(score_grad, q[rows, :])
-        out_q[rows, :] = (dot_nn(score_grad, s["kw"][window, :]) * SCALE).astype(BF)
+        s["dk"][:, window] += dot_nn(qt[:, rows], score_grad)
+        out_q[:, rows] = (dot_nt(s["kw"][:, window], score_grad) * SCALE).astype(BF)
         if b == 1:
-            s["ks"][...] = (s["dk"][0:REACH, :] * SCALE).astype(BF)
+            s["ks"][...] = (s["dk"][:, 0:REACH] * SCALE).astype(BF)
             s["vs"][...] = s["dv"][0:REACH, :].astype(BF)
             send(s["ks"], s["kr"], s["s_k"].at[0], s["s_k"].at[1], before)
             send(s["vs"], s["vr"], s["s_k"].at[2], s["s_k"].at[3], before)
-    out_k[0:REACH, :] = (s["dk"][REACH : 2 * REACH, :] * SCALE).astype(BF)
+    out_k[:, 0:REACH] = (s["dk"][:, REACH : 2 * REACH] * SCALE).astype(BF)
     out_v[0:REACH, :] = s["dv"][REACH : 2 * REACH, :].astype(BF)
     wait(s["kr"], s["s_k"].at[1])
-    out_k[REACH:TOK, :] = (
-        s["dk"][2 * REACH : 3 * REACH, :] * SCALE + s["kr"][...].astype(F32)
+    out_k[:, REACH:TOK] = (
+        s["dk"][:, 2 * REACH : 3 * REACH] * SCALE + s["kr"][...].astype(F32)
     ).astype(BF)
     wait(s["vr"], s["s_k"].at[3])
     out_v[REACH:TOK, :] = (s["dv"][2 * REACH : 3 * REACH, :] + s["vr"][...].astype(F32)).astype(BF)
 
+    for buf in range(2):
+        own_o[buf].wait()
+        wait(s["orr"].at[buf, pl.ds(0, 7)], s["s_o"].at[2 + buf])
+        got = s["orr"][buf].reshape(N_EXP * SLOTS, 512)
+        out_res[:, 1024 * buf : 1024 * buf + 512] = dot_nn(s["tin"][...], got).astype(BF)
+        out_res[:, 1024 * buf + 512 : 1024 * buf + 1024] = dot_nn(s["tdy"][...], got).astype(BF)
+
     wait(s["w"].at[pl.ds(0, 63)], s["s_wsend"])
     wait(s["opf"].at[pl.ds(0, 7)], s["s_op_s"])
-    wait(keys_in.at[pl.ds(0, REACH)], s["s_halo_s"].at[0])
+    wait(keys_in.at[:, pl.ds(0, REACH)], s["s_halo_s"].at[0])
     wait(values_in.at[pl.ds(0, REACH)], s["s_halo_s"].at[1])
     wait(s["segh"], s["s_halo_s"].at[2])
     wait(s["xs"].at[pl.ds(0, 7)], s["s_x"].at[0])
+    wait(s["auxs"].at[pl.ds(0, 7)], s["s_aux"].at[0])
+    wait(s["placer"].at[pl.ds(0, 7)], s["s_aux"].at[2])
     for buf in range(2):
         wait(os.at[buf, pl.ds(0, 7)], s["s_o"].at[buf])
     wait(s["hs"].at[pl.ds(0, 7)], s["s_h"].at[0])
@@ -456,29 +560,28 @@
     residual, out_grad, norm_gain, expert_ids, route_weights, gate_up, down_proj, out_proj,
     queries, keys_in, values_in, segments,
 ):
-    down = down_proj.reshape(12, D)
-    packed = jnp.concatenate([down[:, :1536], down[:, 1536:].reshape(4, 1536)], axis=0)
-    share = jnp.concatenate([gate_up.reshape(64, FF), packed[:, :FF], packed[:, FF:]], axis=0)
     vm = pl.BlockSpec(memory_space=pltpu.VMEM)
     hbm = pl.BlockSpec(memory_space=pl.ANY)
-    return pl.pallas_call(
+    residual_grad, query_grad, key_grad, value_grad = pl.pallas_call(
         body,
         out_shape=(
             jax.ShapeDtypeStruct((TOK_DEV, D), BF),
-            jax.ShapeDtypeStruct((TOK, QK), BF),
-            jax.ShapeDtypeStruct((TOK, QK), BF),
+            jax.ShapeDtypeStruct((QK, TOK), BF),
+            jax.ShapeDtypeStruct((QK, TOK), BF),
             jax.ShapeDtypeStruct((TOK, VD), BF),
         ),
-        in_specs=[hbm] * 4 + [vm] * 7,
+        in_specs=[hbm] * 4 + [vm] * 8,
         out_specs=(vm,) * 4,
         scratch_shapes=list(scratch().values()),
         compiler_params=pltpu.CompilerParams(
             collective_id=0, has_side_effects=True, vmem_limit_bytes=60 * 1024 * 1024
         ),
     )(
-        share, out_proj, keys_in, values_in, residual, out_grad, norm_gain.reshape(1, D),
-        expert_ids, route_weights, segments.reshape(8, 128), queries,
+        gate_up.reshape(64, FF), out_proj, keys_in.T, values_in, down_proj.reshape(12, D),
+        residual, out_grad, norm_gain.reshape(16, 128), expert_ids.T, route_weights.T,
+        segments.reshape(8, 128), queries.T,
     )
+    return residual_grad, query_grad.T, key_grad.T, value_grad
 
 
 def solution(mesh):

time: 127 us -> 104 us (0.82)
  Pallas kernels: 112 us -> 97.2 us
  local copies, waits for them, and re-layouts: 11.9 us -> 4.86 us
  other arithmetic: 1.59 us -> 0 us
    pallas_call x1, Pallas kernels: 112 us -> 97.2 us  [shards(): pl.pallas_call(body, out_shape=(jax.ShapeDtypeStruct((TOK_DEV, D), BF), j...]
    pallas_call x2 -> x0, local copies, waits for them, and re-layouts: 2.97 us -> none  [shards(): pl.pallas_call(body, out_shape=(jax.ShapeDtypeStruct((TOK_DEV, D), BF), j...]
    concatenate x2 -> x0, other arithmetic: 1.59 us -> none  [the longest x1 1.57 us: shards(): jnp.concatenate([gate_up.reshape(64, FF), packed[:, :FF], packed[:, FF:]]...]
    slice x2 -> x0, local copies, waits for them, and re-layouts: 1.52 us -> none  [the longest x1 0.8 us: shards(): down[:, :1536]]
    reshape x2 -> x0, local copies, waits for them, and re-layouts: 1.36 us -> none  [the longest x1 1.34 us: shards(): norm_gain.reshape(1, D)]
    unnamed x18 -> x10, local copies, waits for them, and re-layouts: 6.06 us -> 4.86 us
where the time goes in v2:
time: 104 us; the launch traced here: 103 us
  Pallas kernels  97.2 us (93%)
  local copies, waits for them, and re-layouts  4.86 us (5%)
    pallas_call x1, Pallas kernels, shards(): pl.pallas_call(body, out_shape=(jax.ShapeDtypeStruct((TOK_DEV, D), BF), j...  97.2 us
    unnamed x10, local copies, waits for them, and re-layouts  4.86 us

profile of v2, /device:TPU:57, one launch (start us, length us, event | category | flops | bytes accessed | tf_op | source)
XLA Modules:
  0.0 102.7 jit_solution(17899635791510072097)
XLA Ops:
  0.6 97.2 %shard_map.147 = (bf16[128,2048]{1,0:T(8,128)(2,1)}, bf16[192,1024]{1,0:T(8,128)(2,1)}, bf16[192,1024]{1,0:T(8,128)(2,1)}, bf16[1024,128]{1,0:T(8,128)(2,1)}) custom-call(bf16[64,768]{1,0:T(8,128)(2,1)} %bitcast.14, bf16[128,2048]{1,0:T(8,128)(2,1)} %op_in.1, bf16[192,1024]{1,0:T(8,128)(2,1)} %bitcast.10, bf16[1024,128]{1,0:T(8,128)(2,1)} %values_in.1, ...), custom_call_target="tpu_custom_call" | custom-call | tf_op jit(solution)/shard_map/pallas_call | solution.py:565
  97.8 0.0 copy-start.1
  97.8 1.9 %copy.20 = bf16[128,2048]{1,0:T(8,128)(2,1)} copy(bf16[128,2048]{1,0:T(8,128)(2,1)} %get-tuple-element.16) | data formatting | bytes 1048576
  99.7 0.0 copy-done.1
  99.7 0.0 copy-start
  99.7 0.7 copy.21
  100.5 0.4 copy-done
  100.9 0.0 copy-start.2
  100.9 0.7 copy.22
  101.6 0.3 copy-done.2
  102.0 0.7 copy.23
Async XLA Ops:
  97.8 1.9 %copy-start.1 = (bf16[192,1024]{1,0:T(8,128)(2,1)S(1)}, bf16[192,1024]{1,0:T(8,128)(2,1)}, u32[]{:S(2)}) copy-start(bf16[192,1024]{1,0:T(8,128)(2,1)} %get-tuple-element.9) | copy-start | bytes 1179652
  99.7 1.1 %copy-start = (bf16[192,1024]{1,0:T(8,128)(2,1)S(1)}, bf16[192,1024]{1,0:T(8,128)(2,1)}, u32[]{:S(2)}) copy-start(bf16[192,1024]{1,0:T(8,128)(2,1)} %get-tuple-element.10) | copy-start | bytes 1179652
  100.9 1.1 %copy-start.2 = (bf16[1024,128]{1,0:T(8,128)(2,1)S(1)}, bf16[1024,128]{1,0:T(8,128)(2,1)}, u32[]{:S(2)}) copy-start(bf16[1024,128]{1,0:T(8,128)(2,1)} %get-tuple-element.19) | copy-start | bytes 786436

commit v3 on v2

--- a/solution.py
+++ b/solution.py
@@ -81,12 +81,14 @@
         att=vm((TOK, VD), F32),
         dk=vm((QK, REACH + TOK), F32),
         dv=vm((REACH + TOK, VD), F32),
-        ks=vm((QK, REACH), BF),
-        vs=vm((REACH, VD), BF),
-        kr=vm((QK, REACH), BF),
-        vr=vm((REACH, VD), BF),
+        ks=vm((2, QK, QB), BF),
+        vs=vm((2, QB, VD), BF),
+        kr=vm((2, QK, QB), BF),
+        vr=vm((2, QB, VD), BF),
         s_local=dma((10,)),
         s_wsend=dma,
+        s_z=dma((2,)),
+        s_half=dma((2,)),
         s_w=dma((NH * NY,)),
         s_cross=dma((NH,)),
         s_halo_s=dma((3,)),
@@ -97,7 +99,7 @@
         s_aux=dma((4,)),
         s_o=dma((4,)),
         s_h=dma((2,)),
-        s_k=dma((4,)),
+        s_k=dma((8,)),
     )
 
 
@@ -159,17 +161,17 @@
     w_in = s["w"].at[ctx]
     pl.semaphore_wait(barrier, len(partners))
 
-    def wsend(src, hh, yy, dev):
+    def wsend(src, hh, yy, dev, sem=None):
         j = at(hh, yy)
-        send(src, s["w"].at[j], s["s_wsend"], s["s_w"].at[hh * NY + yy], dev)
+        send(src, s["w"].at[j], s["s_wsend"] if sem is None else sem, s["s_w"].at[hh * NY + yy], dev)
 
     def cross(src, hh, yy):
         send(src, s["w"].at[at(hh, yy)], s["s_wsend"], s["s_cross"].at[hh], sibling)
 
     wsend(w_in, h, y, up)
     wsend(w_in, h, y, down)
-    for dev in zs:
-        wsend(w_in, h, y, dev)
+    wsend(w_in, h, y, zs[0], s["s_z"].at[0])
+    wsend(w_in, h, y, zs[2], s["s_z"].at[1])
     cross(w_in, h, y)
     half = pl.ds(64 * c, 64)
     send(op_in.at[half], s["opf"].at[me, half], s["s_op_s"], s["s_op_r"].at[0], lmate)
@@ -248,6 +250,10 @@
     def tables():
         s["tin"][...] = jnp.transpose(hit_in)
         s["tdy"][...] = jnp.transpose(hit_dy)
+
+    def clear():
+        s["dk"][...] = jnp.zeros((QK, REACH + TOK), F32)
+        s["dv"][...] = jnp.zeros((REACH + TOK, VD), F32)
 
     def places_ready():
         own[2].wait()
@@ -323,15 +329,28 @@
     def arrive(d, k, way):
         hh = (h + k) % NH
         yy = (y + NY - way * d) % NY
-        if d + k > 0:
+        j = at(hh, yy)
+        src = s["w"].at[j]
+        if d == 4 and k == 1:
+            for part in range(2):
+                wait(s["w"].at[0, pl.ds(0, 48)], s["s_half"].at[part])
+        else:
             wait(s["w"].at[0], s["s_w"].at[hh * NY + yy])
-            src = s["w"].at[at(hh, yy)]
-            if d == 0:
-                wsend(src, hh, yy, up)
-                wsend(src, hh, yy, down)
-            elif d < 3 or (d == 3 and (k < 2) == (way == 1)):
-                wsend(src, hh, yy, up if way == 1 else down)
-            cross(src, hh, yy)
+        if d == 0:
+            wsend(src, hh, yy, up)
+            wsend(src, hh, yy, down)
+        elif d < 3 or (d == 3 and k != 1 and (k == 0) == (way == 1)):
+            wsend(src, hh, yy, up if way == 1 else down)
+        elif d == 3 and k == 1:
+            part = 0 if way == 1 else 1
+            rows = pl.ds(48 * part, 48)
+            send(src.at[rows], s["w"].at[j, rows], s["s_wsend"], s["s_half"].at[part], up if way == 1 else down)
+        cross(src, hh, yy)
+
+    def far_send():
+        wait(s["w"].at[0], s["s_z"].at[0])
+        wait(s["w"].at[0], s["s_z"].at[1])
+        wsend(w_in, h, y, zs[1])
 
     def experts(k):
         hh = (h + k) % NH
@@ -373,7 +392,7 @@
     normalize()
     steps = [
         (1, 0, -1), (1, 0, 1),
-        lambda: dispatch(0, 512),
+        lambda: dispatch(0, 512), far_send,
         (0, 1, 0), (0, 3, 0),
         lambda: dispatch(1024, 1536), dispatch_send,
         (2, 0, -1), (2, 0, 1),
@@ -381,7 +400,7 @@
         (1, 1, -1), (1, 1, 1), (0, 2, 0),
         tables, lambda: selection(0),
         (1, 3, -1), (1, 3, 1),
-        lambda: selection(1), op_pass,
+        lambda: selection(1), op_pass, clear,
         (3, 0, -1), (3, 0, 1),
         halo_ready, lambda: forward(0),
         (2, 1, -1), (2, 1, 1),
@@ -390,17 +409,17 @@
         lambda: forward(2), lambda: op_cross(1, l),
         (2, 3, -1), (2, 3, 1),
         lambda: forward(3),
-        (3, 1, -1), (4, 0, 1),
+        (3, 1, -1), (3, 1, 1), (4, 0, 1),
         places_ready, lambda: [place_table(src) for src in range(4)],
-        (2, 2, -1), (3, 1, 1),
+        (2, 2, -1), (2, 2, 1),
         lambda: [place_table(src) for src in range(4, 8)], lambda: selection(2),
-        (2, 2, 1), (3, 3, -1),
+        (3, 3, -1), (3, 3, 1),
         lambda: selection(3), rows_ready, lambda: experts(0),
-        (3, 2, -1), (3, 3, 1),
+        (3, 2, -1), (3, 2, 1),
         lambda: op_cross(2, 1 - l),
         (4, 1, 1), (4, 3, -1),
         lambda: experts(1),
-        (3, 2, 1), (4, 2, -1),
+        (4, 2, -1),
         lambda: experts(3), lambda: experts(2),
     ]
     for step in steps:
@@ -473,6 +492,12 @@
                 [o0[128:192].reshape(N_EXP, 8, 256), o1[128:192].reshape(N_EXP, 8, 256)], axis=1
             )
             os[buf, :, 32:48, cols] = tail.astype(BF)
+
+    def home_send(buf, e):
+        send(os.at[buf, e], s["orr"].at[buf, me], s["s_o"].at[buf], s["s_o"].at[2 + buf], (ctx, e))
+
+    home_send(0, 2 * ((x + 2) % 4))
+    home_send(0, 2 * ((x + 2) % 4) + 1)
 
     local[1].wait()
     wait(s["opf"].at[pl.ds(0, 7), pl.ds(0, 64)], s["s_op_r"].at[3])
@@ -493,15 +518,17 @@
             own_h = pltpu.make_async_copy(s["hs"].at[me], s["hr"].at[me], s["s_local"].at[7])
             own_h.start()
 
+
+    wait(s["hs"].at[pl.ds(0, 7)], s["s_h"].at[0])
     own_o = []
     for buf in range(2):
-        for dev in exps:
-            send(os.at[buf, dev[1]], s["orr"].at[buf, me], s["s_o"].at[buf], s["s_o"].at[2 + buf], dev)
+        for step in (2, 1, 3, 0):
+            for e in (2 * ((x + step) % 4), 2 * ((x + step) % 4) + 1) if step else (lmate[1],):
+                if buf or step != 2:
+                    home_send(buf, e)
         copy = pltpu.make_async_copy(os.at[buf, me], s["orr"].at[buf, me], s["s_local"].at[5 + buf])
         copy.start()
         own_o.append(copy)
-    s["dk"][...] = jnp.zeros((QK, REACH + TOK), F32)
-    s["dv"][...] = jnp.zeros((REACH + TOK, VD), F32)
     own_h.wait()
     wait(s["hr"].at[pl.ds(0, 7)], s["s_h"].at[1])
 
@@ -520,20 +547,19 @@
         s["dv"][window, :] += dot_nn(s["plt"][b], grad)
         s["dk"][:, window] += dot_nn(qt[:, rows], score_grad)
         out_q[:, rows] = (dot_nt(s["kw"][:, window], score_grad) * SCALE).astype(BF)
-        if b == 1:
-            s["ks"][...] = (s["dk"][:, 0:REACH] * SCALE).astype(BF)
-            s["vs"][...] = s["dv"][0:REACH, :].astype(BF)
-            send(s["ks"], s["kr"], s["s_k"].at[0], s["s_k"].at[1], before)
-            send(s["vs"], s["vr"], s["s_k"].at[2], s["s_k"].at[3], before)
+        if b < 2:
+            s["ks"][b] = (s["dk"][:, rows] * SCALE).astype(BF)
+            s["vs"][b] = s["dv"][rows, :].astype(BF)
+            send(s["ks"].at[b], s["kr"].at[b], s["s_k"].at[b], s["s_k"].at[2 + b], before)
+            send(s["vs"].at[b], s["vr"].at[b], s["s_k"].at[4 + b], s["s_k"].at[6 + b], before)
     out_k[:, 0:REACH] = (s["dk"][:, REACH : 2 * REACH] * SCALE).astype(BF)
     out_v[0:REACH, :] = s["dv"][REACH : 2 * REACH, :].astype(BF)
-    wait(s["kr"], s["s_k"].at[1])
-    out_k[:, REACH:TOK] = (
-        s["dk"][:, 2 * REACH : 3 * REACH] * SCALE + s["kr"][...].astype(F32)
-    ).astype(BF)
-    wait(s["vr"], s["s_k"].at[3])
-    out_v[REACH:TOK, :] = (s["dv"][2 * REACH : 3 * REACH, :] + s["vr"][...].astype(F32)).astype(BF)
-
+    for b in range(2):
+        rows, mine = pl.ds(REACH + QB * b, QB), pl.ds(2 * REACH + QB * b, QB)
+        wait(s["kr"].at[b], s["s_k"].at[2 + b])
+        out_k[:, rows] = (s["dk"][:, mine] * SCALE + s["kr"][b].astype(F32)).astype(BF)
+        wait(s["vr"].at[b], s["s_k"].at[6 + b])
+        out_v[rows, :] = (s["dv"][mine, :] + s["vr"][b].astype(F32)).astype(BF)
     for buf in range(2):
         own_o[buf].wait()
         wait(s["orr"].at[buf, pl.ds(0, 7)], s["s_o"].at[2 + buf])
@@ -541,7 +567,7 @@
         out_res[:, 1024 * buf : 1024 * buf + 512] = dot_nn(s["tin"][...], got).astype(BF)
         out_res[:, 1024 * buf + 512 : 1024 * buf + 1024] = dot_nn(s["tdy"][...], got).astype(BF)
 
-    wait(s["w"].at[pl.ds(0, 63)], s["s_wsend"])
+    wait(s["w"].at[pl.ds(0, 61)], s["s_wsend"])
     wait(s["opf"].at[pl.ds(0, 7)], s["s_op_s"])
     wait(keys_in.at[:, pl.ds(0, REACH)], s["s_halo_s"].at[0])
     wait(values_in.at[pl.ds(0, REACH)], s["s_halo_s"].at[1])
@@ -551,9 +577,22 @@
     wait(s["placer"].at[pl.ds(0, 7)], s["s_aux"].at[2])
     for buf in range(2):
         wait(os.at[buf, pl.ds(0, 7)], s["s_o"].at[buf])
-    wait(s["hs"].at[pl.ds(0, 7)], s["s_h"].at[0])
-    wait(s["ks"], s["s_k"].at[0])
-    wait(s["vs"], s["s_k"].at[2])
+    for b in range(2):
+        wait(s["ks"].at[b], s["s_k"].at[b])
+        wait(s["vs"].at[b], s["s_k"].at[4 + b])
+
+
+def hand_over(a, b, c, d, oa, ob, oc, od, va, vb, vc, vd, sem):
+    triples = ((a, va, oa), (b, vb, ob), (c, vc, oc), (d, vd, od))
+    into = [pltpu.make_async_copy(t[0], t[1], sem.at[i]) for i, t in enumerate(triples)]
+    out = [pltpu.make_async_copy(t[1], t[2], sem.at[4 + i]) for i, t in enumerate(triples)]
+    for copy in into:
+        copy.start()
+    for i in range(4):
+        into[i].wait()
+        out[i].start()
+    for copy in out:
+        copy.wait()
 
 
 def shards(
@@ -562,7 +601,7 @@
 ):
     vm = pl.BlockSpec(memory_space=pltpu.VMEM)
     hbm = pl.BlockSpec(memory_space=pl.ANY)
-    residual_grad, query_grad, key_grad, value_grad = pl.pallas_call(
+    results = pl.pallas_call(
         body,
         out_shape=(
             jax.ShapeDtypeStruct((TOK_DEV, D), BF),
@@ -581,6 +620,13 @@
         residual, out_grad, norm_gain.reshape(16, 128), expert_ids.T, route_weights.T,
         segments.reshape(8, 128), queries.T,
     )
+    residual_grad, query_grad, key_grad, value_grad = pl.pallas_call(
+        hand_over,
+        out_shape=tuple(jax.ShapeDtypeStruct(r.shape, r.dtype) for r in results),
+        in_specs=[hbm] * 4,
+        out_specs=(hbm,) * 4,
+        scratch_shapes=[pltpu.VMEM(r.shape, r.dtype) for r in results] + [pltpu.SemaphoreType.DMA((8,))],
+    )(*results)
     return residual_grad, query_grad.T, key_grad.T, value_grad
 
 

time: 104 us -> 100 us (0.962)
  local copies, waits for them, and re-layouts: 4.86 us -> 0 us
    unnamed x10 -> x0, local copies, waits for them, and re-layouts: 4.86 us -> none
    pallas_call x0 -> x1, Pallas kernels: none -> 2.25 us  [shards(): pl.pallas_call(hand_over, out_shape=tuple((jax.ShapeDtypeStruct(r.shape,...]
    pallas_call x1, Pallas kernels: 97.2 us -> 95.7 us  [shards(): pl.pallas_call(body, out_shape=(jax.ShapeDtypeStruct((TOK_DEV, D), BF), j...]
where the time goes in v3:
time: 100 us; the launch traced here: 98.7 us
  Pallas kernels  97.9 us (98%)
    pallas_call x1, Pallas kernels, shards(): pl.pallas_call(body, out_shape=(jax.ShapeDtypeStruct((TOK_DEV, D), BF), j...  95.7 us
    pallas_call x1, Pallas kernels, shards(): pl.pallas_call(hand_over, out_shape=tuple((jax.ShapeDtypeStruct(r.shape,...  2.25 us

profile of v3, /device:TPU:57, one launch (start us, length us, event | category | flops | bytes accessed | tf_op | source)
XLA Modules:
  0.0 98.7 jit_solution(1766359661379760672)
XLA Ops:
  0.6 95.7 %shard_map.147 = (bf16[128,2048]{1,0:T(8,128)(2,1)}, bf16[192,1024]{1,0:T(8,128)(2,1)}, bf16[192,1024]{1,0:T(8,128)(2,1)}, bf16[1024,128]{1,0:T(8,128)(2,1)}) custom-call(bf16[64,768]{1,0:T(8,128)(2,1)} %bitcast.12, bf16[128,2048]{1,0:T(8,128)(2,1)} %op_in.1, bf16[192,1024]{1,0:T(8,128)(2,1)} %bitcast.10, bf16[1024,128]{1,0:T(8,128)(2,1)} %values_in.1, ...), custom_call_target="tpu_custom_call" | custom-call | tf_op jit(solution)/shard_map/pallas_call | solution.py:604
  96.3 2.2 %shard_map.148 = (bf16[128,2048]{1,0:T(8,128)(2,1)}, bf16[192,1024]{1,0:T(8,128)(2,1)}, bf16[192,1024]{1,0:T(8,128)(2,1)}, bf16[1024,128]{1,0:T(8,128)(2,1)}) custom-call(bf16[128,2048]{1,0:T(8,128)(2,1)} %get-tuple-element.12.a, bf16[192,1024]{1,0:T(8,128)(2,1)} %get-tuple-element.13.b, bf16[192,1024]{1,0:T(8,128)(2,1)} %get-tuple-element.14.c, ...), custom_call_target="tpu_custom_call" | custom-call | tf_op jit(solution)/shard_map/pallas_call | solution.py:623

commit v4 on v3

--- a/solution.py
+++ b/solution.py
@@ -174,15 +174,8 @@
     wsend(w_in, h, y, zs[2], s["s_z"].at[1])
     cross(w_in, h, y)
     half = pl.ds(64 * c, 64)
-    send(op_in.at[half], s["opf"].at[me, half], s["s_op_s"], s["s_op_r"].at[0], lmate)
     for dev in xmates:
         send(op_in.at[half], s["opf"].at[me, half], s["s_op_s"], s["s_op_r"].at[1], dev)
-    send(keys_in.at[:, pl.ds(REACH, REACH)], s["kw"].at[:, pl.ds(0, REACH)],
-         s["s_halo_s"].at[0], s["s_halo_r"].at[0], after)
-    send(values_in.at[pl.ds(REACH, REACH)], s["vw"].at[pl.ds(0, REACH)],
-         s["s_halo_s"].at[1], s["s_halo_r"].at[1], after)
-    send(seg, s["segh"], s["s_halo_s"].at[2], s["s_halo_r"].at[2], after)
-
     gain_rows = gain[...].astype(F32)
     gain_f = jnp.concatenate([gain_rows[i : i + 1, :] for i in range(16)], axis=1)
 
@@ -351,6 +344,15 @@
         wait(s["w"].at[0], s["s_z"].at[0])
         wait(s["w"].at[0], s["s_z"].at[1])
         wsend(w_in, h, y, zs[1])
+        send(op_in.at[half], s["opf"].at[me, half], s["s_op_s"], s["s_op_r"].at[0], lmate)
+
+    def halo_send():
+        send(keys_in.at[:, pl.ds(REACH, REACH)], s["kw"].at[:, pl.ds(0, REACH)],
+             s["s_halo_s"].at[0], s["s_halo_r"].at[0], after)
+        send(values_in.at[pl.ds(REACH, REACH)], s["vw"].at[pl.ds(0, REACH)],
+             s["s_halo_s"].at[1], s["s_halo_r"].at[1], after)
+        send(seg, s["segh"], s["s_halo_s"].at[2], s["s_halo_r"].at[2], after)
+
 
     def experts(k):
         hh = (h + k) % NH
@@ -396,23 +398,23 @@
         (0, 1, 0), (0, 3, 0),
         lambda: dispatch(1024, 1536), dispatch_send,
         (2, 0, -1), (2, 0, 1),
-        side_send,
+        halo_send, side_send,
         (1, 1, -1), (1, 1, 1), (0, 2, 0),
         tables, lambda: selection(0),
         (1, 3, -1), (1, 3, 1),
-        lambda: selection(1), op_pass, clear,
+        lambda: selection(1), clear,
         (3, 0, -1), (3, 0, 1),
+        places_ready, lambda: [place_table(src) for src in range(4)],
+        (2, 1, -1), (2, 1, 1),
+        op_pass, lambda: [place_table(src) for src in range(4, 8)],
+        (1, 2, -1), (1, 2, 1),
         halo_ready, lambda: forward(0),
-        (2, 1, -1), (2, 1, 1),
-        lambda: forward(1),
-        (1, 2, -1), (1, 2, 1),
-        lambda: forward(2), lambda: op_cross(1, l),
         (2, 3, -1), (2, 3, 1),
-        lambda: forward(3),
+        lambda: forward(1), lambda: op_cross(1, l),
         (3, 1, -1), (3, 1, 1), (4, 0, 1),
-        places_ready, lambda: [place_table(src) for src in range(4)],
+        lambda: forward(2),
         (2, 2, -1), (2, 2, 1),
-        lambda: [place_table(src) for src in range(4, 8)], lambda: selection(2),
+        lambda: forward(3), lambda: selection(2),
         (3, 3, -1), (3, 3, 1),
         lambda: selection(3), rows_ready, lambda: experts(0),
         (3, 2, -1), (3, 2, 1),

time: 100 us -> 115 us (1.15)
  Pallas kernels: 97.9 us -> 113 us
    pallas_call x1, Pallas kernels: 95.7 us -> 111 us  [shards(): pl.pallas_call(body, out_shape=(jax.ShapeDtypeStruct((TOK_DEV, D), BF), j...]
where the time goes in v4:
time: 115 us; the launch traced here: 114 us
  Pallas kernels  113 us (98%)
    pallas_call x1, Pallas kernels, shards(): pl.pallas_call(body, out_shape=(jax.ShapeDtypeStruct((TOK_DEV, D), BF), j...  111 us

profile of v4, /device:TPU:57, one launch (start us, length us, event | category | flops | bytes accessed | tf_op | source)
XLA Modules:
  0.0 114.2 jit_solution(14812141817225735700)
XLA Ops:
  0.6 111.2 %shard_map.147 = (bf16[128,2048]{1,0:T(8,128)(2,1)}, bf16[192,1024]{1,0:T(8,128)(2,1)}, bf16[192,1024]{1,0:T(8,128)(2,1)}, bf16[1024,128]{1,0:T(8,128)(2,1)}) custom-call(bf16[64,768]{1,0:T(8,128)(2,1)} %bitcast.12, bf16[128,2048]{1,0:T(8,128)(2,1)} %op_in.1, bf16[192,1024]{1,0:T(8,128)(2,1)} %bitcast.10, bf16[1024,128]{1,0:T(8,128)(2,1)} %values_in.1, ...), custom_call_target="tpu_custom_call" | custom-call | tf_op jit(solution)/shard_map/pallas_call | solution.py:606
  111.8 2.2 %shard_map.148 = (bf16[128,2048]{1,0:T(8,128)(2,1)}, bf16[192,1024]{1,0:T(8,128)(2,1)}, bf16[192,1024]{1,0:T(8,128)(2,1)}, bf16[1024,128]{1,0:T(8,128)(2,1)}) custom-call(bf16[128,2048]{1,0:T(8,128)(2,1)} %get-tuple-element.12.a, bf16[192,1024]{1,0:T(8,128)(2,1)} %get-tuple-element.13.b, bf16[192,1024]{1,0:T(8,128)(2,1)} %get-tuple-element.14.c, ...), custom_call_target="tpu_custom_call" | custom-call | tf_op jit(solution)/shard_map/pallas_call | solution.py:625
